TPU v7x, 256 devices: a whole 4x4x8 slice. The times are simulated.
256 devices in a mesh: blk: 32 (over z_lo, x, core), head: 8 (over z_hi, y).
Axes of the slice: x: 4, y: 4, z: 8 (z_hi: 2, z_lo: 4; z = z_hi * 4 + z_lo), core: 2. Of those that a mesh axis runs over, the one named last changes fastest.
Arguments:
- queries: bfloat16 [4096, 8192], P('blk', 'head'), may hold values from -6 to 6
- key_matrix: bfloat16 [4096, 1024], P(('blk', 'head')), may hold values from -6 to 6
- value_matrix: bfloat16 [4096, 1024], P(('blk', 'head')), may hold values from -6 to 6
- output: bfloat16 [4096, 8192], P('blk', 'head'), may hold values from -6 to 6
- grad_out: bfloat16 [4096, 8192], P('blk', 'head'), may hold values from -6 to 6
- log_norm: bfloat16 [4096, 64], P('blk', 'head'), may hold values from 3 to 6
- doc_ids: int32 [4096], replicated, may hold values from 0 to 5, never falling along the last dimension, each value on 1 to 2048 neighbouring positions
- block_order: int32 [64], replicated, may hold values from 0 to 63, each once
Outputs:
- grad_query: bfloat16 [4096, 8192], P('blk', 'head')
- key_gradient_rows: bfloat16 [4096, 1024], P(('blk', 'head'))
- value_gradient_rows: bfloat16 [4096, 1024], P(('blk', 'head'))
Inputs may be any that keep to these rules, and one draw needn't show every extreme that they name: `doc_ids`: never falls along the sequence; each document holds at most 2048 positions, one exactly 2048. `block_order`: each block number once.
All inputs are finite; a program needn't handle non-finite values.
Results may differ from a plain program's by a relative error of at most 0.0058.
Values may be sent and summed in bfloat16 or wider, within the bound.
A program may use at most 64 MiB of HBM per device.

v0:
```python
import math

import jax
import jax.numpy as jnp
from jax import lax
from jax.sharding import PartitionSpec as P

HEAD_WIDTH = 128


def shifted(array, axis, by):
    length = lax.axis_size(axis)
    return lax.ppermute(array, axis, [(i, (i + by) % length) for i in range(length)])


def span_layout(first_span, span_count, block_order, doc_ids, block_rows):
    firsts = lax.dynamic_slice_in_dim(block_order, 2 * first_span, 2 * span_count)
    offsets = jnp.arange(block_rows, dtype=jnp.int32)
    positions = (firsts[:, None] * block_rows + offsets[None, :]).reshape(-1)
    documents = jnp.concatenate(
        [
            lax.dynamic_slice_in_dim(doc_ids, firsts[which_block] * block_rows, block_rows)
            for which_block in range(2 * span_count)
        ]
    )
    return (positions, documents)


def tile_grads(query_tiles, grad_tiles, norm_tiles, delta_tiles, key_block, value_block, allowed):
    softmax_scale = 1.0 / math.sqrt(HEAD_WIDTH)
    scores = (
        jnp.einsum("qhgd,khd->hgqk", query_tiles, key_block, preferred_element_type=jnp.float32)
        * softmax_scale
    )
    weights = jnp.where(allowed, jnp.exp(scores - norm_tiles), 0.0)
    grad_weights = jnp.einsum(
        "qhgd,khd->hgqk", grad_tiles, value_block, preferred_element_type=jnp.float32
    )
    grad_scores = weights * (grad_weights - delta_tiles)
    weights_b = weights.astype(jnp.bfloat16)
    scores_b = grad_scores.astype(jnp.bfloat16)
    grad_value_part = jnp.einsum(
        "hgqk,qhgd->khd", weights_b, grad_tiles, preferred_element_type=jnp.float32
    )
    grad_key_part = (
        jnp.einsum("hgqk,qhgd->khd", scores_b, query_tiles, preferred_element_type=jnp.float32)
        * softmax_scale
    )
    grad_query_part = (
        jnp.einsum("hgqk,khd->qhgd", scores_b, key_block, preferred_element_type=jnp.float32)
        * softmax_scale
    )
    return (grad_query_part, grad_key_part, grad_value_part)


def body(queries, key_matrix, value_matrix, output, grad_out, log_norm, doc_ids, block_order):
    keys_here, values_here = (
        lax.all_to_all(key_matrix, "head", split_axis=1, concat_axis=0, tiled=True),
        lax.all_to_all(value_matrix, "head", split_axis=1, concat_axis=0, tiled=True),
    )
    span_rows = queries.shape[0]
    block_rows = span_rows // 2
    kv_heads = keys_here.shape[1] // HEAD_WIDTH
    q_heads = log_norm.shape[1]
    group_width = q_heads // kv_heads
    query_tiles = queries.reshape(span_rows, kv_heads, group_width, HEAD_WIDTH)
    grad_tiles = grad_out.reshape(span_rows, kv_heads, group_width, HEAD_WIDTH)
    row_delta = jnp.sum(
        grad_tiles.astype(jnp.float32)
        * output.reshape(span_rows, kv_heads, group_width, HEAD_WIDTH).astype(jnp.float32),
        axis=-1,
    )
    delta_tiles = jnp.transpose(row_delta, (1, 2, 0))[..., None]
    norm_tiles = jnp.transpose(
        log_norm.astype(jnp.float32).reshape(span_rows, kv_heads, group_width), (1, 2, 0)
    )[..., None]
    heads_of_keys = keys_here.reshape(span_rows, kv_heads, HEAD_WIDTH)
    heads_of_values = values_here.reshape(span_rows, kv_heads, HEAD_WIDTH)
    cycle_size = lax.axis_size("blk")
    own_index = lax.axis_index("blk")
    query_pos, query_docs = span_layout(own_index, 1, block_order, doc_ids, block_rows)

    def grads_for(first_span, span_count, key_block, value_block):
        key_pos, key_docs = span_layout(first_span, span_count, block_order, doc_ids, block_rows)
        allowed = (key_pos[None, :] <= query_pos[:, None]) & (
            key_docs[None, :] == query_docs[:, None]
        )
        return tile_grads(
            query_tiles, grad_tiles, norm_tiles, delta_tiles, key_block, value_block, allowed
        )

    zero_query = jnp.zeros((span_rows, kv_heads, group_width, HEAD_WIDTH), jnp.float32)
    zero_keys = jnp.zeros((span_rows, kv_heads, HEAD_WIDTH), jnp.float32)

    def cycle_turn(turn_index, state_tuple):
        key_block, value_block, key_gradient, value_gradient, grad_query = state_tuple
        source = (own_index - turn_index) % cycle_size
        query_part, key_part, value_part = grads_for(source, 1, key_block, value_block)
        key_block, value_block = shifted((key_block, value_block), "blk", 1)
        key_gradient, value_gradient = shifted(
            (key_gradient + key_part, value_gradient + value_part), "blk", 1
        )
        return (key_block, value_block, key_gradient, value_gradient, grad_query + query_part)

    def two_turns(pair_index, state_tuple):
        state_tuple = cycle_turn(2 * pair_index, state_tuple)
        return cycle_turn(2 * pair_index + 1, state_tuple)

    start_state = (heads_of_keys, heads_of_values, zero_keys, zero_keys, zero_query)
    final_state = lax.fori_loop(0, cycle_size // 2, two_turns, start_state)
    key_gradient, value_gradient, grad_query = (final_state[2], final_state[3], final_state[4])
    query_out = grad_query.astype(jnp.bfloat16).reshape(span_rows, q_heads * HEAD_WIDTH)
    key_out = key_gradient.astype(jnp.bfloat16).reshape(span_rows, kv_heads * HEAD_WIDTH)
    value_out = value_gradient.astype(jnp.bfloat16).reshape(span_rows, kv_heads * HEAD_WIDTH)
    key_back, value_back = (
        lax.all_to_all(key_out, "head", split_axis=0, concat_axis=1, tiled=True),
        lax.all_to_all(value_out, "head", split_axis=0, concat_axis=1, tiled=True),
    )
    return (query_out, key_back, value_back)


def solution(mesh):
    placed = (
        P("blk", "head"),
        P(("blk", "head"), None),
        P(("blk", "head"), None),
        P("blk", "head"),
        P("blk", "head"),
        P("blk", "head"),
        P(),
        P(),
    )
    return jax.shard_map(
        body,
        mesh=mesh,
        in_specs=placed,
        out_specs=(P("blk", "head"), P(("blk", "head"), None), P(("blk", "head"), None)),
        check_vma=False,
    )
```

profile of v0, /device:TPU:8, one launch (start us, length us, event | category | flops | bytes accessed | tf_op | source)
XLA Modules:
  0.0 420.8 jit_solution(12105651539524169218)
XLA Ops:
  2.0 11.7 %all-to-all-start = ((bf16[16,8,128]{2,0,1:T(8,128)(2,1)}), bf16[16,8,128]{2,0,1:T(8,128)(2,1)S(1)}, u32[]{:S(2)}, u32[]{:S(2)}) async-start(bf16[16,8,128]{2,0,1:T(8,128)(2,1)} %copy_bitcast_fusion.4), calls=%async_computation | async-start | bytes 65536 | tf_op jit(solution)/shard_map/all_to_all | solution.py:58
  17.6 1.1 copy.44
  22.4 9.1 %all-to-all-start.1 = ((bf16[16,8,128]{2,0,1:T(8,128)(2,1)}), bf16[16,8,128]{2,0,1:T(8,128)(2,1)S(1)}, u32[]{:S(2)}, u32[]{:S(2)}) async-start(bf16[16,8,128]{2,0,1:T(8,128)(2,1)} %copy_bitcast_fusion.3), calls=%async_computation.1 | async-start | bytes 65536 | tf_op jit(solution)/shard_map/all_to_all | solution.py:59
  31.6 8.6 %all-to-all-done.1 = bf16[16,8,128]{2,0,1:T(8,128)(2,1)S(1)} async-done(((bf16[16,8,128]{2,0,1:T(8,128)(2,1)}), bf16[16,8,128]{2,0,1:T(8,128)(2,1)S(1)}, u32[]{:S(2)}, u32[]{:S(2)}) %all-to-all-start.1) | async-done | bytes 32800 | tf_op jit(solution)/shard_map/all_to_all | solution.py:59
  40.2 352.4 %while.24 = (s32[]{:T(128)}, bf16[128,1,128]{2,0,1:T(8,128)(2,1)S(1)}, bf16[128,1,128]{2,0,1:T(8,128)(2,1)S(1)}, f32[128,1,128]{2,0,1:T(8,128)S(1)}, f32[128,1,1...) while((s32[]{:T(128)}, ...), condition=%wide.region_2.3_spmd.clone, body=%wide.region_1.2_spmd.clone.sunk | while | flops 338232000 | bytes 11301557 | solution.py:110
  40.3 1.6 collective-permute-start
  47.9 1.6 collective-permute-start.6
  49.9 1.3 collective-permute-start.1
  51.7 3.5 collective-permute-done.4
  57.5 5.6 %collective-permute-done.5 = f32[128,1,128]{2,0,1:T(8,128)S(1)} collective-permute-done((f32[128,1,128]{2,0,1:T(8,128)S(1)}, f32[128,1,128]{2,0,1:T(8,128)S(1)}, u32[]{:S(2)}, u32[]{:S(2)}) %collective-permute-start.5) | collective-permute-done | bytes 65568 | tf_op jit(solution)/shard_map/while/body/eval_jaxpr/ppermute | solution.py:13
  70.1 1.0 collective-permute-done.2
  71.9 5.2 %collective-permute-done.4 = f32[128,1,128]{2,0,1:T(8,128)S(1)} collective-permute-done((f32[128,1,128]{2,0,1:T(8,128)S(1)}, f32[128,1,128]{2,0,1:T(8,128)S(1)}, u32[]{:S(2)}, u32[]{:S(2)}) %collective-permute-start.4) | collective-permute-done | bytes 65568 | tf_op jit(solution)/shard_map/while/body/eval_jaxpr/ppermute | solution.py:13
  78.6 6.4 %collective-permute-done.5 = f32[128,1,128]{2,0,1:T(8,128)S(1)} collective-permute-done((f32[128,1,128]{2,0,1:T(8,128)S(1)}, f32[128,1,128]{2,0,1:T(8,128)S(1)}, u32[]{:S(2)}, u32[]{:S(2)}) %collective-permute-start.5) | collective-permute-done | bytes 65568 | tf_op jit(solution)/shard_map/while/body/eval_jaxpr/ppermute | solution.py:13
  93.8 5.2 %collective-permute-done.4 = f32[128,1,128]{2,0,1:T(8,128)S(1)} collective-permute-done((f32[128,1,128]{2,0,1:T(8,128)S(1)}, f32[128,1,128]{2,0,1:T(8,128)S(1)}, u32[]{:S(2)}, u32[]{:S(2)}) %collective-permute-start.4) | collective-permute-done | bytes 65568 | tf_op jit(solution)/shard_map/while/body/eval_jaxpr/ppermute | solution.py:13
  100.6 6.4 %collective-permute-done.5 = f32[128,1,128]{2,0,1:T(8,128)S(1)} collective-permute-done((f32[128,1,128]{2,0,1:T(8,128)S(1)}, f32[128,1,128]{2,0,1:T(8,128)S(1)}, u32[]{:S(2)}, u32[]{:S(2)}) %collective-permute-start.5) | collective-permute-done | bytes 65568 | tf_op jit(solution)/shard_map/while/body/eval_jaxpr/ppermute | solution.py:13
  113.9 1.0 collective-permute-done.2
  115.7 5.2 %collective-permute-done.4 = f32[128,1,128]{2,0,1:T(8,128)S(1)} collective-permute-done((f32[128,1,128]{2,0,1:T(8,128)S(1)}, f32[128,1,128]{2,0,1:T(8,128)S(1)}, u32[]{:S(2)}, u32[]{:S(2)}) %collective-permute-start.4) | collective-permute-done | bytes 65568 | tf_op jit(solution)/shard_map/while/body/eval_jaxpr/ppermute | solution.py:13
  122.5 6.4 %collective-permute-done.5 = f32[128,1,128]{2,0,1:T(8,128)S(1)} collective-permute-done((f32[128,1,128]{2,0,1:T(8,128)S(1)}, f32[128,1,128]{2,0,1:T(8,128)S(1)}, u32[]{:S(2)}, u32[]{:S(2)}) %collective-permute-start.5) | collective-permute-done | bytes 65568 | tf_op jit(solution)/shard_map/while/body/eval_jaxpr/ppermute | solution.py:13
  137.7 5.2 %collective-permute-done.4 = f32[128,1,128]{2,0,1:T(8,128)S(1)} collective-permute-done((f32[128,1,128]{2,0,1:T(8,128)S(1)}, f32[128,1,128]{2,0,1:T(8,128)S(1)}, u32[]{:S(2)}, u32[]{:S(2)}) %collective-permute-start.4) | collective-permute-done | bytes 65568 | tf_op jit(solution)/shard_map/while/body/eval_jaxpr/ppermute | solution.py:13
  144.4 6.4 %collective-permute-done.5 = f32[128,1,128]{2,0,1:T(8,128)S(1)} collective-permute-done((f32[128,1,128]{2,0,1:T(8,128)S(1)}, f32[128,1,128]{2,0,1:T(8,128)S(1)}, u32[]{:S(2)}, u32[]{:S(2)}) %collective-permute-start.5) | collective-permute-done | bytes 65568 | tf_op jit(solution)/shard_map/while/body/eval_jaxpr/ppermute | solution.py:13
  159.6 5.2 %collective-permute-done.4 = f32[128,1,128]{2,0,1:T(8,128)S(1)} collective-permute-done((f32[128,1,128]{2,0,1:T(8,128)S(1)}, f32[128,1,128]{2,0,1:T(8,128)S(1)}, u32[]{:S(2)}, u32[]{:S(2)}) %collective-permute-start.4) | collective-permute-done | bytes 65568 | tf_op jit(solution)/shard_map/while/body/eval_jaxpr/ppermute | solution.py:13
  166.4 6.4 %collective-permute-done.5 = f32[128,1,128]{2,0,1:T(8,128)S(1)} collective-permute-done((f32[128,1,128]{2,0,1:T(8,128)S(1)}, f32[128,1,128]{2,0,1:T(8,128)S(1)}, u32[]{:S(2)}, u32[]{:S(2)}) %collective-permute-start.5) | collective-permute-done | bytes 65568 | tf_op jit(solution)/shard_map/while/body/eval_jaxpr/ppermute | solution.py:13
  181.5 5.2 %collective-permute-done.4 = f32[128,1,128]{2,0,1:T(8,128)S(1)} collective-permute-done((f32[128,1,128]{2,0,1:T(8,128)S(1)}, f32[128,1,128]{2,0,1:T(8,128)S(1)}, u32[]{:S(2)}, u32[]{:S(2)}) %collective-permute-start.4) | collective-permute-done | bytes 65568 | tf_op jit(solution)/shard_map/while/body/eval_jaxpr/ppermute | solution.py:13
  188.3 6.4 %collective-permute-done.5 = f32[128,1,128]{2,0,1:T(8,128)S(1)} collective-permute-done((f32[128,1,128]{2,0,1:T(8,128)S(1)}, f32[128,1,128]{2,0,1:T(8,128)S(1)}, u32[]{:S(2)}, u32[]{:S(2)}) %collective-permute-start.5) | collective-permute-done | bytes 65568 | tf_op jit(solution)/shard_map/while/body/eval_jaxpr/ppermute | solution.py:13
  203.4 5.2 %collective-permute-done.4 = f32[128,1,128]{2,0,1:T(8,128)S(1)} collective-permute-done((f32[128,1,128]{2,0,1:T(8,128)S(1)}, f32[128,1,128]{2,0,1:T(8,128)S(1)}, u32[]{:S(2)}, u32[]{:S(2)}) %collective-permute-start.4) | collective-permute-done | bytes 65568 | tf_op jit(solution)/shard_map/while/body/eval_jaxpr/ppermute | solution.py:13
  210.2 6.4 %collective-permute-done.5 = f32[128,1,128]{2,0,1:T(8,128)S(1)} collective-permute-done((f32[128,1,128]{2,0,1:T(8,128)S(1)}, f32[128,1,128]{2,0,1:T(8,128)S(1)}, u32[]{:S(2)}, u32[]{:S(2)}) %collective-permute-start.5) | collective-permute-done | bytes 65568 | tf_op jit(solution)/shard_map/while/body/eval_jaxpr/ppermute | solution.py:13
  225.3 5.2 %collective-permute-done.4 = f32[128,1,128]{2,0,1:T(8,128)S(1)} collective-permute-done((f32[128,1,128]{2,0,1:T(8,128)S(1)}, f32[128,1,128]{2,0,1:T(8,128)S(1)}, u32[]{:S(2)}, u32[]{:S(2)}) %collective-permute-start.4) | collective-permute-done | bytes 65568 | tf_op jit(solution)/shard_map/while/body/eval_jaxpr/ppermute | solution.py:13
  232.1 6.3 %collective-permute-done.5 = f32[128,1,128]{2,0,1:T(8,128)S(1)} collective-permute-done((f32[128,1,128]{2,0,1:T(8,128)S(1)}, f32[128,1,128]{2,0,1:T(8,128)S(1)}, u32[]{:S(2)}, u32[]{:S(2)}) %collective-permute-start.5) | collective-permute-done | bytes 65568 | tf_op jit(solution)/shard_map/while/body/eval_jaxpr/ppermute | solution.py:13
  247.2 5.2 %collective-permute-done.4 = f32[128,1,128]{2,0,1:T(8,128)S(1)} collective-permute-done((f32[128,1,128]{2,0,1:T(8,128)S(1)}, f32[128,1,128]{2,0,1:T(8,128)S(1)}, u32[]{:S(2)}, u32[]{:S(2)}) %collective-permute-start.4) | collective-permute-done | bytes 65568 | tf_op jit(solution)/shard_map/while/body/eval_jaxpr/ppermute | solution.py:13
  254.0 6.4 %collective-permute-done.5 = f32[128,1,128]{2,0,1:T(8,128)S(1)} collective-permute-done((f32[128,1,128]{2,0,1:T(8,128)S(1)}, f32[128,1,128]{2,0,1:T(8,128)S(1)}, u32[]{:S(2)}, u32[]{:S(2)}) %collective-permute-start.5) | collective-permute-done | bytes 65568 | tf_op jit(solution)/shard_map/while/body/eval_jaxpr/ppermute | solution.py:13
  269.1 5.2 %collective-permute-done.4 = f32[128,1,128]{2,0,1:T(8,128)S(1)} collective-permute-done((f32[128,1,128]{2,0,1:T(8,128)S(1)}, f32[128,1,128]{2,0,1:T(8,128)S(1)}, u32[]{:S(2)}, u32[]{:S(2)}) %collective-permute-start.4) | collective-permute-done | bytes 65568 | tf_op jit(solution)/shard_map/while/body/eval_jaxpr/ppermute | solution.py:13
  275.9 6.4 %collective-permute-done.5 = f32[128,1,128]{2,0,1:T(8,128)S(1)} collective-permute-done((f32[128,1,128]{2,0,1:T(8,128)S(1)}, f32[128,1,128]{2,0,1:T(8,128)S(1)}, u32[]{:S(2)}, u32[]{:S(2)}) %collective-permute-start.5) | collective-permute-done | bytes 65568 | tf_op jit(solution)/shard_map/while/body/eval_jaxpr/ppermute | solution.py:13
  291.0 5.3 %collective-permute-done.4 = f32[128,1,128]{2,0,1:T(8,128)S(1)} collective-permute-done((f32[128,1,128]{2,0,1:T(8,128)S(1)}, f32[128,1,128]{2,0,1:T(8,128)S(1)}, u32[]{:S(2)}, u32[]{:S(2)}) %collective-permute-start.4) | collective-permute-done | bytes 65568 | tf_op jit(solution)/shard_map/while/body/eval_jaxpr/ppermute | solution.py:13
  297.8 6.4 %collective-permute-done.5 = f32[128,1,128]{2,0,1:T(8,128)S(1)} collective-permute-done((f32[128,1,128]{2,0,1:T(8,128)S(1)}, f32[128,1,128]{2,0,1:T(8,128)S(1)}, u32[]{:S(2)}, u32[]{:S(2)}) %collective-permute-start.5) | collective-permute-done | bytes 65568 | tf_op jit(solution)/shard_map/while/body/eval_jaxpr/ppermute | solution.py:13
  313.0 5.2 %collective-permute-done.4 = f32[128,1,128]{2,0,1:T(8,128)S(1)} collective-permute-done((f32[128,1,128]{2,0,1:T(8,128)S(1)}, f32[128,1,128]{2,0,1:T(8,128)S(1)}, u32[]{:S(2)}, u32[]{:S(2)}) %collective-permute-start.4) | collective-permute-done | bytes 65568 | tf_op jit(solution)/shard_map/while/body/eval_jaxpr/ppermute | solution.py:13
  319.8 6.4 %collective-permute-done.5 = f32[128,1,128]{2,0,1:T(8,128)S(1)} collective-permute-done((f32[128,1,128]{2,0,1:T(8,128)S(1)}, f32[128,1,128]{2,0,1:T(8,128)S(1)}, u32[]{:S(2)}, u32[]{:S(2)}) %collective-permute-start.5) | collective-permute-done | bytes 65568 | tf_op jit(solution)/shard_map/while/body/eval_jaxpr/ppermute | solution.py:13
  333.1 1.0 collective-permute-done.2
  334.9 5.2 %collective-permute-done.4 = f32[128,1,128]{2,0,1:T(8,128)S(1)} collective-permute-done((f32[128,1,128]{2,0,1:T(8,128)S(1)}, f32[128,1,128]{2,0,1:T(8,128)S(1)}, u32[]{:S(2)}, u32[]{:S(2)}) %collective-permute-start.4) | collective-permute-done | bytes 65568 | tf_op jit(solution)/shard_map/while/body/eval_jaxpr/ppermute | solution.py:13
  341.7 6.4 %collective-permute-done.5 = f32[128,1,128]{2,0,1:T(8,128)S(1)} collective-permute-done((f32[128,1,128]{2,0,1:T(8,128)S(1)}, f32[128,1,128]{2,0,1:T(8,128)S(1)}, u32[]{:S(2)}, u32[]{:S(2)}) %collective-permute-start.5) | collective-permute-done | bytes 65568 | tf_op jit(solution)/shard_map/while/body/eval_jaxpr/ppermute | solution.py:13
  355.0 1.0 collective-permute-done.2
  356.8 5.2 %collective-permute-done.4 = f32[128,1,128]{2,0,1:T(8,128)S(1)} collective-permute-done((f32[128,1,128]{2,0,1:T(8,128)S(1)}, f32[128,1,128]{2,0,1:T(8,128)S(1)}, u32[]{:S(2)}, u32[]{:S(2)}) %collective-permute-start.4) | collective-permute-done | bytes 65568 | tf_op jit(solution)/shard_map/while/body/eval_jaxpr/ppermute | solution.py:13
  363.6 6.3 %collective-permute-done.5 = f32[128,1,128]{2,0,1:T(8,128)S(1)} collective-permute-done((f32[128,1,128]{2,0,1:T(8,128)S(1)}, f32[128,1,128]{2,0,1:T(8,128)S(1)}, u32[]{:S(2)}, u32[]{:S(2)}) %collective-permute-start.5) | collective-permute-done | bytes 65568 | tf_op jit(solution)/shard_map/while/body/eval_jaxpr/ppermute | solution.py:13
  378.7 5.2 %collective-permute-done.4 = f32[128,1,128]{2,0,1:T(8,128)S(1)} collective-permute-done((f32[128,1,128]{2,0,1:T(8,128)S(1)}, f32[128,1,128]{2,0,1:T(8,128)S(1)}, u32[]{:S(2)}, u32[]{:S(2)}) %collective-permute-start.4) | collective-permute-done | bytes 65568 | tf_op jit(solution)/shard_map/while/body/eval_jaxpr/ppermute | solution.py:13
  385.5 6.4 %collective-permute-done.5 = f32[128,1,128]{2,0,1:T(8,128)S(1)} collective-permute-done((f32[128,1,128]{2,0,1:T(8,128)S(1)}, f32[128,1,128]{2,0,1:T(8,128)S(1)}, u32[]{:S(2)}, u32[]{:S(2)}) %collective-permute-start.5) | collective-permute-done | bytes 65568 | tf_op jit(solution)/shard_map/while/body/eval_jaxpr/ppermute | solution.py:13
  393.2 4.7 %all-to-all-start.2 = ((bf16[8,16,128]{2,1,0:T(8,128)(2,1)}), bf16[8,16,128]{2,1,0:T(8,128)(2,1)S(1)}, u32[]{:S(2)}, u32[]{:S(2)}) async-start(bf16[8,16,128]{2,1,0:T(8,128)(2,1)} %bitcast.15), calls=%async_computation.2 | async-start | bytes 65536 | tf_op jit(solution)/shard_map/all_to_all | solution.py:116
  399.5 7.2 %all-to-all-done.2 = bf16[8,16,128]{2,1,0:T(8,128)(2,1)S(1)} async-done(((bf16[8,16,128]{2,1,0:T(8,128)(2,1)}), bf16[8,16,128]{2,1,0:T(8,128)(2,1)S(1)}, u32[]{:S(2)}, u32[]{:S(2)}) %all-to-all-start.2) | async-done | bytes 32800 | tf_op jit(solution)/shard_map/all_to_all | solution.py:116
  406.7 4.7 %all-to-all-start.3 = ((bf16[8,16,128]{2,1,0:T(8,128)(2,1)}), bf16[8,16,128]{2,1,0:T(8,128)(2,1)S(1)}, u32[]{:S(2)}, u32[]{:S(2)}) async-start(bf16[8,16,128]{2,1,0:T(8,128)(2,1)} %bitcast.17), calls=%async_computation.3 | async-start | bytes 65536 | tf_op jit(solution)/shard_map/all_to_all | solution.py:117
  412.0 8.1 %all-to-all-done.3 = bf16[8,16,128]{2,1,0:T(8,128)(2,1)S(1)} async-done(((bf16[8,16,128]{2,1,0:T(8,128)(2,1)}), bf16[8,16,128]{2,1,0:T(8,128)(2,1)S(1)}, u32[]{:S(2)}, u32[]{:S(2)}) %all-to-all-start.3) | async-done | bytes 32800 | tf_op jit(solution)/shard_map/all_to_all | solution.py:117
  (588 shorter events, 128.2 us)
Async XLA Ops:
  2.0 20.4 %all-to-all-start = ((bf16[16,8,128]{2,0,1:T(8,128)(2,1)}), bf16[16,8,128]{2,0,1:T(8,128)(2,1)S(1)}, u32[]{:S(2)}, u32[]{:S(2)}) async-start(bf16[16,8,128]{2,0,1:T(8,128)(2,1)} %copy_bitcast_fusion.4), calls=%async_computation | async-start | bytes 65536 | tf_op jit(solution)/shard_map/all_to_all | solution.py:58
  22.4 17.8 %all-to-all-start.1 = ((bf16[16,8,128]{2,0,1:T(8,128)(2,1)}), bf16[16,8,128]{2,0,1:T(8,128)(2,1)S(1)}, u32[]{:S(2)}, u32[]{:S(2)}) async-start(bf16[16,8,128]{2,0,1:T(8,128)(2,1)} %copy_bitcast_fusion.3), calls=%async_computation.1 | async-start | bytes 65536 | tf_op jit(solution)/shard_map/all_to_all | solution.py:59
  40.2 9.5 %collective-permute-start.2 = (bf16[128,1,128]{2,0,1:T(8,128)(2,1)S(1)}, bf16[128,1,128]{2,0,1:T(8,128)(2,1)S(1)}, u32[]{:S(2)}, u32[]{:S(2)}) collective-permute-start(bf16[128,1,128]{2,0,1:T(8,128)(2,1)S(1)} %get-tuple-element.661), channel_id=1, source_target_pairs={{0,8},{8,16},{16,24},{24,32},{32,40},{40,48},{48,56},{56,64},{64,7... | collective-permute-start | bytes 98312 | tf_op jit(solution)/shard_map/while/body/eval_jaxpr/ppermute | solution.py:13
  40.3 9.6 %collective-permute-start = (bf16[128,1,128]{2,0,1:T(8,128)(2,1)S(1)}, bf16[128,1,128]{2,0,1:T(8,128)(2,1)S(1)}, u32[]{:S(2)}, u32[]{:S(2)}) collective-permute-start(bf16[128,1,128]{2,0,1:T(8,128)(2,1)S(1)} %get-tuple-element.660), channel_id=1, source_target_pairs={{0,8},{8,16},{16,24},{24,32},{32,40},{40,48},{48,56},{56,64},{64,7... | collective-permute-start | bytes 98312 | tf_op jit(solution)/shard_map/while/body/eval_jaxpr/ppermute | solution.py:13
  47.5 7.7 %collective-permute-start.4 = (f32[128,1,128]{2,0,1:T(8,128)S(1)}, f32[128,1,128]{2,0,1:T(8,128)S(1)}, u32[]{:S(2)}, u32[]{:S(2)}) collective-permute-start(f32[128,1,128]{2,0,1:T(8,128)S(1)} %fusion.118), channel_id=1, source_target_pairs={{0,8},{8,16},{16,24},{24,32},{32,40},{40,48},{48,56},{56,64},{64,7... | collective-permute-start | bytes 196616 | tf_op jit(solution)/shard_map/while/body/eval_jaxpr/ppermute | solution.py:13
  47.9 8.0 %collective-permute-start.6 = (f32[128,1,128]{2,0,1:T(8,128)S(1)}, f32[128,1,128]{2,0,1:T(8,128)S(1)}, u32[]{:S(2)}, u32[]{:S(2)}) collective-permute-start(f32[128,1,128]{2,0,1:T(8,128)S(1)} %fusion.122), channel_id=1, source_target_pairs={{0,8},{8,16},{16,24},{24,32},{32,40},{40,48},{48,56},{56,64},{64,7... | collective-permute-start | bytes 196616 | tf_op jit(solution)/shard_map/while/body/eval_jaxpr/ppermute | solution.py:13
  55.4 7.7 %collective-permute-start.5 = (f32[128,1,128]{2,0,1:T(8,128)S(1)}, f32[128,1,128]{2,0,1:T(8,128)S(1)}, u32[]{:S(2)}, u32[]{:S(2)}) collective-permute-start(f32[128,1,128]{2,0,1:T(8,128)S(1)} %fusion.121), channel_id=1, source_target_pairs={{0,8},{8,16},{16,24},{24,32},{32,40},{40,48},{48,56},{56,64},{64,7... | collective-permute-start | bytes 196616 | tf_op jit(solution)/shard_map/while/body/eval_jaxpr/ppermute | solution.py:13
  56.1 7.7 %collective-permute-start.7 = (f32[128,1,128]{2,0,1:T(8,128)S(1)}, f32[128,1,128]{2,0,1:T(8,128)S(1)}, u32[]{:S(2)}, u32[]{:S(2)}) collective-permute-start(f32[128,1,128]{2,0,1:T(8,128)S(1)} %fusion.123), channel_id=1, source_target_pairs={{0,8},{8,16},{16,24},{24,32},{32,40},{40,48},{48,56},{56,64},{64,7... | collective-permute-start | bytes 196616 | tf_op jit(solution)/shard_map/while/body/eval_jaxpr/ppermute | solution.py:13
  69.4 7.7 %collective-permute-start.4 = (f32[128,1,128]{2,0,1:T(8,128)S(1)}, f32[128,1,128]{2,0,1:T(8,128)S(1)}, u32[]{:S(2)}, u32[]{:S(2)}) collective-permute-start(f32[128,1,128]{2,0,1:T(8,128)S(1)} %fusion.118), channel_id=1, source_target_pairs={{0,8},{8,16},{16,24},{24,32},{32,40},{40,48},{48,56},{56,64},{64,7... | collective-permute-start | bytes 196616 | tf_op jit(solution)/shard_map/while/body/eval_jaxpr/ppermute | solution.py:13
  69.7 8.1 %collective-permute-start.6 = (f32[128,1,128]{2,0,1:T(8,128)S(1)}, f32[128,1,128]{2,0,1:T(8,128)S(1)}, u32[]{:S(2)}, u32[]{:S(2)}) collective-permute-start(f32[128,1,128]{2,0,1:T(8,128)S(1)} %fusion.122), channel_id=1, source_target_pairs={{0,8},{8,16},{16,24},{24,32},{32,40},{40,48},{48,56},{56,64},{64,7... | collective-permute-start | bytes 196616 | tf_op jit(solution)/shard_map/while/body/eval_jaxpr/ppermute | solution.py:13
  78.0 7.7 %collective-permute-start.7 = (f32[128,1,128]{2,0,1:T(8,128)S(1)}, f32[128,1,128]{2,0,1:T(8,128)S(1)}, u32[]{:S(2)}, u32[]{:S(2)}) collective-permute-start(f32[128,1,128]{2,0,1:T(8,128)S(1)} %fusion.123), channel_id=1, source_target_pairs={{0,8},{8,16},{16,24},{24,32},{32,40},{40,48},{48,56},{56,64},{64,7... | collective-permute-start | bytes 196616 | tf_op jit(solution)/shard_map/while/body/eval_jaxpr/ppermute | solution.py:13
  91.3 7.7 %collective-permute-start.4 = (f32[128,1,128]{2,0,1:T(8,128)S(1)}, f32[128,1,128]{2,0,1:T(8,128)S(1)}, u32[]{:S(2)}, u32[]{:S(2)}) collective-permute-start(f32[128,1,128]{2,0,1:T(8,128)S(1)} %fusion.118), channel_id=1, source_target_pairs={{0,8},{8,16},{16,24},{24,32},{32,40},{40,48},{48,56},{56,64},{64,7... | collective-permute-start | bytes 196616 | tf_op jit(solution)/shard_map/while/body/eval_jaxpr/ppermute | solution.py:13
  91.6 8.1 %collective-permute-start.6 = (f32[128,1,128]{2,0,1:T(8,128)S(1)}, f32[128,1,128]{2,0,1:T(8,128)S(1)}, u32[]{:S(2)}, u32[]{:S(2)}) collective-permute-start(f32[128,1,128]{2,0,1:T(8,128)S(1)} %fusion.122), channel_id=1, source_target_pairs={{0,8},{8,16},{16,24},{24,32},{32,40},{40,48},{48,56},{56,64},{64,7... | collective-permute-start | bytes 196616 | tf_op jit(solution)/shard_map/while/body/eval_jaxpr/ppermute | solution.py:13
  113.2 7.7 %collective-permute-start.4 = (f32[128,1,128]{2,0,1:T(8,128)S(1)}, f32[128,1,128]{2,0,1:T(8,128)S(1)}, u32[]{:S(2)}, u32[]{:S(2)}) collective-permute-start(f32[128,1,128]{2,0,1:T(8,128)S(1)} %fusion.118), channel_id=1, source_target_pairs={{0,8},{8,16},{16,24},{24,32},{32,40},{40,48},{48,56},{56,64},{64,7... | collective-permute-start | bytes 196616 | tf_op jit(solution)/shard_map/while/body/eval_jaxpr/ppermute | solution.py:13
  113.5 8.1 %collective-permute-start.6 = (f32[128,1,128]{2,0,1:T(8,128)S(1)}, f32[128,1,128]{2,0,1:T(8,128)S(1)}, u32[]{:S(2)}, u32[]{:S(2)}) collective-permute-start(f32[128,1,128]{2,0,1:T(8,128)S(1)} %fusion.122), channel_id=1, source_target_pairs={{0,8},{8,16},{16,24},{24,32},{32,40},{40,48},{48,56},{56,64},{64,7... | collective-permute-start | bytes 196616 | tf_op jit(solution)/shard_map/while/body/eval_jaxpr/ppermute | solution.py:13
  121.2 7.7 %collective-permute-start.5 = (f32[128,1,128]{2,0,1:T(8,128)S(1)}, f32[128,1,128]{2,0,1:T(8,128)S(1)}, u32[]{:S(2)}, u32[]{:S(2)}) collective-permute-start(f32[128,1,128]{2,0,1:T(8,128)S(1)} %fusion.121), channel_id=1, source_target_pairs={{0,8},{8,16},{16,24},{24,32},{32,40},{40,48},{48,56},{56,64},{64,7... | collective-permute-start | bytes 196616 | tf_op jit(solution)/shard_map/while/body/eval_jaxpr/ppermute | solution.py:13
  121.9 7.7 %collective-permute-start.7 = (f32[128,1,128]{2,0,1:T(8,128)S(1)}, f32[128,1,128]{2,0,1:T(8,128)S(1)}, u32[]{:S(2)}, u32[]{:S(2)}) collective-permute-start(f32[128,1,128]{2,0,1:T(8,128)S(1)} %fusion.123), channel_id=1, source_target_pairs={{0,8},{8,16},{16,24},{24,32},{32,40},{40,48},{48,56},{56,64},{64,7... | collective-permute-start | bytes 196616 | tf_op jit(solution)/shard_map/while/body/eval_jaxpr/ppermute | solution.py:13
  135.2 7.7 %collective-permute-start.4 = (f32[128,1,128]{2,0,1:T(8,128)S(1)}, f32[128,1,128]{2,0,1:T(8,128)S(1)}, u32[]{:S(2)}, u32[]{:S(2)}) collective-permute-start(f32[128,1,128]{2,0,1:T(8,128)S(1)} %fusion.118), channel_id=1, source_target_pairs={{0,8},{8,16},{16,24},{24,32},{32,40},{40,48},{48,56},{56,64},{64,7... | collective-permute-start | bytes 196616 | tf_op jit(solution)/shard_map/while/body/eval_jaxpr/ppermute | solution.py:13
  135.5 8.1 %collective-permute-start.6 = (f32[128,1,128]{2,0,1:T(8,128)S(1)}, f32[128,1,128]{2,0,1:T(8,128)S(1)}, u32[]{:S(2)}, u32[]{:S(2)}) collective-permute-start(f32[128,1,128]{2,0,1:T(8,128)S(1)} %fusion.122), channel_id=1, source_target_pairs={{0,8},{8,16},{16,24},{24,32},{32,40},{40,48},{48,56},{56,64},{64,7... | collective-permute-start | bytes 196616 | tf_op jit(solution)/shard_map/while/body/eval_jaxpr/ppermute | solution.py:13
  143.1 7.7 %collective-permute-start.5 = (f32[128,1,128]{2,0,1:T(8,128)S(1)}, f32[128,1,128]{2,0,1:T(8,128)S(1)}, u32[]{:S(2)}, u32[]{:S(2)}) collective-permute-start(f32[128,1,128]{2,0,1:T(8,128)S(1)} %fusion.121), channel_id=1, source_target_pairs={{0,8},{8,16},{16,24},{24,32},{32,40},{40,48},{48,56},{56,64},{64,7... | collective-permute-start | bytes 196616 | tf_op jit(solution)/shard_map/while/body/eval_jaxpr/ppermute | solution.py:13
  143.8 7.7 %collective-permute-start.7 = (f32[128,1,128]{2,0,1:T(8,128)S(1)}, f32[128,1,128]{2,0,1:T(8,128)S(1)}, u32[]{:S(2)}, u32[]{:S(2)}) collective-permute-start(f32[128,1,128]{2,0,1:T(8,128)S(1)} %fusion.123), channel_id=1, source_target_pairs={{0,8},{8,16},{16,24},{24,32},{32,40},{40,48},{48,56},{56,64},{64,7... | collective-permute-start | bytes 196616 | tf_op jit(solution)/shard_map/while/body/eval_jaxpr/ppermute | solution.py:13
  157.1 7.7 %collective-permute-start.4 = (f32[128,1,128]{2,0,1:T(8,128)S(1)}, f32[128,1,128]{2,0,1:T(8,128)S(1)}, u32[]{:S(2)}, u32[]{:S(2)}) collective-permute-start(f32[128,1,128]{2,0,1:T(8,128)S(1)} %fusion.118), channel_id=1, source_target_pairs={{0,8},{8,16},{16,24},{24,32},{32,40},{40,48},{48,56},{56,64},{64,7... | collective-permute-start | bytes 196616 | tf_op jit(solution)/shard_map/while/body/eval_jaxpr/ppermute | solution.py:13
  157.5 8.1 %collective-permute-start.6 = (f32[128,1,128]{2,0,1:T(8,128)S(1)}, f32[128,1,128]{2,0,1:T(8,128)S(1)}, u32[]{:S(2)}, u32[]{:S(2)}) collective-permute-start(f32[128,1,128]{2,0,1:T(8,128)S(1)} %fusion.122), channel_id=1, source_target_pairs={{0,8},{8,16},{16,24},{24,32},{32,40},{40,48},{48,56},{56,64},{64,7... | collective-permute-start | bytes 196616 | tf_op jit(solution)/shard_map/while/body/eval_jaxpr/ppermute | solution.py:13
  165.7 7.7 %collective-permute-start.7 = (f32[128,1,128]{2,0,1:T(8,128)S(1)}, f32[128,1,128]{2,0,1:T(8,128)S(1)}, u32[]{:S(2)}, u32[]{:S(2)}) collective-permute-start(f32[128,1,128]{2,0,1:T(8,128)S(1)} %fusion.123), channel_id=1, source_target_pairs={{0,8},{8,16},{16,24},{24,32},{32,40},{40,48},{48,56},{56,64},{64,7... | collective-permute-start | bytes 196616 | tf_op jit(solution)/shard_map/while/body/eval_jaxpr/ppermute | solution.py:13
  179.0 7.7 %collective-permute-start.4 = (f32[128,1,128]{2,0,1:T(8,128)S(1)}, f32[128,1,128]{2,0,1:T(8,128)S(1)}, u32[]{:S(2)}, u32[]{:S(2)}) collective-permute-start(f32[128,1,128]{2,0,1:T(8,128)S(1)} %fusion.118), channel_id=1, source_target_pairs={{0,8},{8,16},{16,24},{24,32},{32,40},{40,48},{48,56},{56,64},{64,7... | collective-permute-start | bytes 196616 | tf_op jit(solution)/shard_map/while/body/eval_jaxpr/ppermute | solution.py:13
  179.3 8.1 %collective-permute-start.6 = (f32[128,1,128]{2,0,1:T(8,128)S(1)}, f32[128,1,128]{2,0,1:T(8,128)S(1)}, u32[]{:S(2)}, u32[]{:S(2)}) collective-permute-start(f32[128,1,128]{2,0,1:T(8,128)S(1)} %fusion.122), channel_id=1, source_target_pairs={{0,8},{8,16},{16,24},{24,32},{32,40},{40,48},{48,56},{56,64},{64,7... | collective-permute-start | bytes 196616 | tf_op jit(solution)/shard_map/while/body/eval_jaxpr/ppermute | solution.py:13
  187.7 7.7 %collective-permute-start.7 = (f32[128,1,128]{2,0,1:T(8,128)S(1)}, f32[128,1,128]{2,0,1:T(8,128)S(1)}, u32[]{:S(2)}, u32[]{:S(2)}) collective-permute-start(f32[128,1,128]{2,0,1:T(8,128)S(1)} %fusion.123), channel_id=1, source_target_pairs={{0,8},{8,16},{16,24},{24,32},{32,40},{40,48},{48,56},{56,64},{64,7... | collective-permute-start | bytes 196616 | tf_op jit(solution)/shard_map/while/body/eval_jaxpr/ppermute | solution.py:13
  200.9 7.7 %collective-permute-start.4 = (f32[128,1,128]{2,0,1:T(8,128)S(1)}, f32[128,1,128]{2,0,1:T(8,128)S(1)}, u32[]{:S(2)}, u32[]{:S(2)}) collective-permute-start(f32[128,1,128]{2,0,1:T(8,128)S(1)} %fusion.118), channel_id=1, source_target_pairs={{0,8},{8,16},{16,24},{24,32},{32,40},{40,48},{48,56},{56,64},{64,7... | collective-permute-start | bytes 196616 | tf_op jit(solution)/shard_map/while/body/eval_jaxpr/ppermute | solution.py:13
  201.2 8.1 %collective-permute-start.6 = (f32[128,1,128]{2,0,1:T(8,128)S(1)}, f32[128,1,128]{2,0,1:T(8,128)S(1)}, u32[]{:S(2)}, u32[]{:S(2)}) collective-permute-start(f32[128,1,128]{2,0,1:T(8,128)S(1)} %fusion.122), channel_id=1, source_target_pairs={{0,8},{8,16},{16,24},{24,32},{32,40},{40,48},{48,56},{56,64},{64,7... | collective-permute-start | bytes 196616 | tf_op jit(solution)/shard_map/while/body/eval_jaxpr/ppermute | solution.py:13
  222.8 7.7 %collective-permute-start.4 = (f32[128,1,128]{2,0,1:T(8,128)S(1)}, f32[128,1,128]{2,0,1:T(8,128)S(1)}, u32[]{:S(2)}, u32[]{:S(2)}) collective-permute-start(f32[128,1,128]{2,0,1:T(8,128)S(1)} %fusion.118), channel_id=1, source_target_pairs={{0,8},{8,16},{16,24},{24,32},{32,40},{40,48},{48,56},{56,64},{64,7... | collective-permute-start | bytes 196616 | tf_op jit(solution)/shard_map/while/body/eval_jaxpr/ppermute | solution.py:13
  223.2 8.1 %collective-permute-start.6 = (f32[128,1,128]{2,0,1:T(8,128)S(1)}, f32[128,1,128]{2,0,1:T(8,128)S(1)}, u32[]{:S(2)}, u32[]{:S(2)}) collective-permute-start(f32[128,1,128]{2,0,1:T(8,128)S(1)} %fusion.122), channel_id=1, source_target_pairs={{0,8},{8,16},{16,24},{24,32},{32,40},{40,48},{48,56},{56,64},{64,7... | collective-permute-start | bytes 196616 | tf_op jit(solution)/shard_map/while/body/eval_jaxpr/ppermute | solution.py:13
  245.1 8.1 %collective-permute-start.6 = (f32[128,1,128]{2,0,1:T(8,128)S(1)}, f32[128,1,128]{2,0,1:T(8,128)S(1)}, u32[]{:S(2)}, u32[]{:S(2)}) collective-permute-start(f32[128,1,128]{2,0,1:T(8,128)S(1)} %fusion.122), channel_id=1, source_target_pairs={{0,8},{8,16},{16,24},{24,32},{32,40},{40,48},{48,56},{56,64},{64,7... | collective-permute-start | bytes 196616 | tf_op jit(solution)/shard_map/while/body/eval_jaxpr/ppermute | solution.py:13
  253.4 7.7 %collective-permute-start.7 = (f32[128,1,128]{2,0,1:T(8,128)S(1)}, f32[128,1,128]{2,0,1:T(8,128)S(1)}, u32[]{:S(2)}, u32[]{:S(2)}) collective-permute-start(f32[128,1,128]{2,0,1:T(8,128)S(1)} %fusion.123), channel_id=1, source_target_pairs={{0,8},{8,16},{16,24},{24,32},{32,40},{40,48},{48,56},{56,64},{64,7... | collective-permute-start | bytes 196616 | tf_op jit(solution)/shard_map/while/body/eval_jaxpr/ppermute | solution.py:13
  266.6 7.7 %collective-permute-start.4 = (f32[128,1,128]{2,0,1:T(8,128)S(1)}, f32[128,1,128]{2,0,1:T(8,128)S(1)}, u32[]{:S(2)}, u32[]{:S(2)}) collective-permute-start(f32[128,1,128]{2,0,1:T(8,128)S(1)} %fusion.118), channel_id=1, source_target_pairs={{0,8},{8,16},{16,24},{24,32},{32,40},{40,48},{48,56},{56,64},{64,7... | collective-permute-start | bytes 196616 | tf_op jit(solution)/shard_map/while/body/eval_jaxpr/ppermute | solution.py:13
  266.9 8.1 %collective-permute-start.6 = (f32[128,1,128]{2,0,1:T(8,128)S(1)}, f32[128,1,128]{2,0,1:T(8,128)S(1)}, u32[]{:S(2)}, u32[]{:S(2)}) collective-permute-start(f32[128,1,128]{2,0,1:T(8,128)S(1)} %fusion.122), channel_id=1, source_target_pairs={{0,8},{8,16},{16,24},{24,32},{32,40},{40,48},{48,56},{56,64},{64,7... | collective-permute-start | bytes 196616 | tf_op jit(solution)/shard_map/while/body/eval_jaxpr/ppermute | solution.py:13
  288.6 7.7 %collective-permute-start.4 = (f32[128,1,128]{2,0,1:T(8,128)S(1)}, f32[128,1,128]{2,0,1:T(8,128)S(1)}, u32[]{:S(2)}, u32[]{:S(2)}) collective-permute-start(f32[128,1,128]{2,0,1:T(8,128)S(1)} %fusion.118), channel_id=1, source_target_pairs={{0,8},{8,16},{16,24},{24,32},{32,40},{40,48},{48,56},{56,64},{64,7... | collective-permute-start | bytes 196616 | tf_op jit(solution)/shard_map/while/body/eval_jaxpr/ppermute | solution.py:13
  288.9 8.1 %collective-permute-start.6 = (f32[128,1,128]{2,0,1:T(8,128)S(1)}, f32[128,1,128]{2,0,1:T(8,128)S(1)}, u32[]{:S(2)}, u32[]{:S(2)}) collective-permute-start(f32[128,1,128]{2,0,1:T(8,128)S(1)} %fusion.122), channel_id=1, source_target_pairs={{0,8},{8,16},{16,24},{24,32},{32,40},{40,48},{48,56},{56,64},{64,7... | collective-permute-start | bytes 196616 | tf_op jit(solution)/shard_map/while/body/eval_jaxpr/ppermute | solution.py:13
  310.5 7.7 %collective-permute-start.4 = (f32[128,1,128]{2,0,1:T(8,128)S(1)}, f32[128,1,128]{2,0,1:T(8,128)S(1)}, u32[]{:S(2)}, u32[]{:S(2)}) collective-permute-start(f32[128,1,128]{2,0,1:T(8,128)S(1)} %fusion.118), channel_id=1, source_target_pairs={{0,8},{8,16},{16,24},{24,32},{32,40},{40,48},{48,56},{56,64},{64,7... | collective-permute-start | bytes 196616 | tf_op jit(solution)/shard_map/while/body/eval_jaxpr/ppermute | solution.py:13
  310.8 8.1 %collective-permute-start.6 = (f32[128,1,128]{2,0,1:T(8,128)S(1)}, f32[128,1,128]{2,0,1:T(8,128)S(1)}, u32[]{:S(2)}, u32[]{:S(2)}) collective-permute-start(f32[128,1,128]{2,0,1:T(8,128)S(1)} %fusion.122), channel_id=1, source_target_pairs={{0,8},{8,16},{16,24},{24,32},{32,40},{40,48},{48,56},{56,64},{64,7... | collective-permute-start | bytes 196616 | tf_op jit(solution)/shard_map/while/body/eval_jaxpr/ppermute | solution.py:13
  319.1 7.7 %collective-permute-start.7 = (f32[128,1,128]{2,0,1:T(8,128)S(1)}, f32[128,1,128]{2,0,1:T(8,128)S(1)}, u32[]{:S(2)}, u32[]{:S(2)}) collective-permute-start(f32[128,1,128]{2,0,1:T(8,128)S(1)} %fusion.123), channel_id=1, source_target_pairs={{0,8},{8,16},{16,24},{24,32},{32,40},{40,48},{48,56},{56,64},{64,7... | collective-permute-start | bytes 196616 | tf_op jit(solution)/shard_map/while/body/eval_jaxpr/ppermute | solution.py:13
  332.4 7.7 %collective-permute-start.4 = (f32[128,1,128]{2,0,1:T(8,128)S(1)}, f32[128,1,128]{2,0,1:T(8,128)S(1)}, u32[]{:S(2)}, u32[]{:S(2)}) collective-permute-start(f32[128,1,128]{2,0,1:T(8,128)S(1)} %fusion.118), channel_id=1, source_target_pairs={{0,8},{8,16},{16,24},{24,32},{32,40},{40,48},{48,56},{56,64},{64,7... | collective-permute-start | bytes 196616 | tf_op jit(solution)/shard_map/while/body/eval_jaxpr/ppermute | solution.py:13
  332.7 8.1 %collective-permute-start.6 = (f32[128,1,128]{2,0,1:T(8,128)S(1)}, f32[128,1,128]{2,0,1:T(8,128)S(1)}, u32[]{:S(2)}, u32[]{:S(2)}) collective-permute-start(f32[128,1,128]{2,0,1:T(8,128)S(1)} %fusion.122), channel_id=1, source_target_pairs={{0,8},{8,16},{16,24},{24,32},{32,40},{40,48},{48,56},{56,64},{64,7... | collective-permute-start | bytes 196616 | tf_op jit(solution)/shard_map/while/body/eval_jaxpr/ppermute | solution.py:13
  354.3 7.7 %collective-permute-start.4 = (f32[128,1,128]{2,0,1:T(8,128)S(1)}, f32[128,1,128]{2,0,1:T(8,128)S(1)}, u32[]{:S(2)}, u32[]{:S(2)}) collective-permute-start(f32[128,1,128]{2,0,1:T(8,128)S(1)} %fusion.118), channel_id=1, source_target_pairs={{0,8},{8,16},{16,24},{24,32},{32,40},{40,48},{48,56},{56,64},{64,7... | collective-permute-start | bytes 196616 | tf_op jit(solution)/shard_map/while/body/eval_jaxpr/ppermute | solution.py:13
  354.6 8.1 %collective-permute-start.6 = (f32[128,1,128]{2,0,1:T(8,128)S(1)}, f32[128,1,128]{2,0,1:T(8,128)S(1)}, u32[]{:S(2)}, u32[]{:S(2)}) collective-permute-start(f32[128,1,128]{2,0,1:T(8,128)S(1)} %fusion.122), channel_id=1, source_target_pairs={{0,8},{8,16},{16,24},{24,32},{32,40},{40,48},{48,56},{56,64},{64,7... | collective-permute-start | bytes 196616 | tf_op jit(solution)/shard_map/while/body/eval_jaxpr/ppermute | solution.py:13
  376.2 7.8 %collective-permute-start.4 = (f32[128,1,128]{2,0,1:T(8,128)S(1)}, f32[128,1,128]{2,0,1:T(8,128)S(1)}, u32[]{:S(2)}, u32[]{:S(2)}) collective-permute-start(f32[128,1,128]{2,0,1:T(8,128)S(1)} %fusion.118), channel_id=1, source_target_pairs={{0,8},{8,16},{16,24},{24,32},{32,40},{40,48},{48,56},{56,64},{64,7... | collective-permute-start | bytes 196616 | tf_op jit(solution)/shard_map/while/body/eval_jaxpr/ppermute | solution.py:13
  376.5 8.2 %collective-permute-start.6 = (f32[128,1,128]{2,0,1:T(8,128)S(1)}, f32[128,1,128]{2,0,1:T(8,128)S(1)}, u32[]{:S(2)}, u32[]{:S(2)}) collective-permute-start(f32[128,1,128]{2,0,1:T(8,128)S(1)} %fusion.122), channel_id=1, source_target_pairs={{0,8},{8,16},{16,24},{24,32},{32,40},{40,48},{48,56},{56,64},{64,7... | collective-permute-start | bytes 196616 | tf_op jit(solution)/shard_map/while/body/eval_jaxpr/ppermute | solution.py:13
  393.2 13.5 %all-to-all-start.2 = ((bf16[8,16,128]{2,1,0:T(8,128)(2,1)}), bf16[8,16,128]{2,1,0:T(8,128)(2,1)S(1)}, u32[]{:S(2)}, u32[]{:S(2)}) async-start(bf16[8,16,128]{2,1,0:T(8,128)(2,1)} %bitcast.15), calls=%async_computation.2 | async-start | bytes 65536 | tf_op jit(solution)/shard_map/all_to_all | solution.py:116
  406.7 13.4 %all-to-all-start.3 = ((bf16[8,16,128]{2,1,0:T(8,128)(2,1)}), bf16[8,16,128]{2,1,0:T(8,128)(2,1)S(1)}, u32[]{:S(2)}, u32[]{:S(2)}) async-start(bf16[8,16,128]{2,1,0:T(8,128)(2,1)} %bitcast.17), calls=%async_computation.3 | async-start | bytes 65536 | tf_op jit(solution)/shard_map/all_to_all | solution.py:117
  (90 other events, 644.4 us)
where the time goes:
time: 423 us; the launch traced here: 421 us
  waiting for transfers between devices  249 us (59%)
  loops' own time  44.2 us (10%)
  starting transfers between devices  40.3 us (10%)
  matrix products  38.2 us (9%)
  local copies, waits for them, and re-layouts  37.5 us (9%)
  other arithmetic  9.58 us (2%)
    ppermute x128, waiting for transfers between devices, shifted(): lax.ppermute(array, axis, [(i, (i + by) % length) for i in range(length)])  224 us
    another operation x1, loops' own time, body(): final_state = lax.fori_loop(0, cycle_size // 2, two_turns, start_state)  44.2 us
    dynamic_slice x17, local copies, waits for them, and re-layouts, span_layout(): lax.dynamic_slice_in_dim(doc_ids, firsts[which_block] * block_rows, block...  14.3 us
    all_to_all x1, starting transfers between devices, body(): lax.all_to_all(key_matrix, 'head', split_axis=1, concat_axis=0, tiled=True)  11.7 us
    slice x17, local copies, waits for them, and re-layouts, span_layout(): firsts[which_block] * block_rows  10.4 us
    ppermute x128, starting transfers between devices, shifted(): lax.ppermute(array, axis, [(i, (i + by) % length) for i in range(length)])  10.1 us
    all_to_all x1, starting transfers between devices, body(): lax.all_to_all(value_matrix, 'head', split_axis=1, concat_axis=0, tiled=T...  9.11 us
    all_to_all x1, waiting for transfers between devices, body(): lax.all_to_all(value_matrix, 'head', split_axis=1, concat_axis=0, tiled=T...  8.63 us
  transfers between devices with their start and end apart: 132, of which 115 were waited for; matrix products, arithmetic and copies ran while one was open for 19% of the time, Pallas kernels for 0%

commit v1 on v0

v1 whole, which is shorter than its diff:
```python
import functools
import math

import jax
import jax.numpy as jnp
from jax import lax
from jax.experimental import pallas as pl
from jax.experimental.pallas import tpu as pltpu
from jax.sharding import PartitionSpec as P

WIDTH = 128
BLOCK = 64
DOCS = 6
TILE = 256
MASKED = -(2.0**17)
ROOT = math.sqrt(WIDTH)
SCALE = 1.0 / ROOT
EXP2_SCALE = SCALE * math.log2(math.e)
BF16 = jnp.bfloat16
F32 = jnp.float32


def root_parts():
    parts, rest = [], ROOT
    for _ in range(3):
        term = _to_bf16(rest)
        parts.append(term)
        rest -= term
    return parts


def _to_bf16(value):
    mantissa, exponent = math.frexp(value)
    return math.ldexp(round(mantissa * 256), exponent - 8)


ROOT_PARTS = root_parts()


def attend_kernel(
    span_ref, order_ref, docs_ref, q_ref, o_ref, g_ref, norm_ref, kv_ref,
    dq_ref, dkv_ref,
    k_pos, v_pos, dk_acc, dv_acc, q_all, g_all, q_turn, g_turn, dq_turn,
):
    rows = 8 * BLOCK
    blocks = k_pos.shape[0] // BLOCK

    def sort_block(i, carry):
        at = pl.multiple_of(order_ref[i] * BLOCK, BLOCK)
        half = pl.multiple_of((i % 2) * BLOCK, BLOCK)
        k_pos[pl.ds(at, BLOCK), :] = kv_ref[i // 2, 0, pl.ds(half, BLOCK), :]
        v_pos[pl.ds(at, BLOCK), :] = kv_ref[i // 2, 1, pl.ds(half, BLOCK), :]
        return carry

    lax.fori_loop(0, blocks, sort_block, 0, unroll=4)
    dk_acc[...] = jnp.zeros_like(dk_acc)
    dv_acc[...] = jnp.zeros_like(dv_acc)

    docs = docs_ref[...]
    starts = [jnp.sum((docs < d).astype(jnp.int32)) for d in range(1, DOCS)]

    lane = lax.broadcasted_iota(jnp.int32, (BLOCK, WIDTH), 1)
    row = lax.broadcasted_iota(jnp.int32, (BLOCK, WIDTH), 0)
    one_hot = (lane == row).astype(F32)
    norm_lane = (lane >= BLOCK) & (lane < BLOCK + 3)

    tile_lane = lax.broadcasted_iota(jnp.int32, (TILE, WIDTH), 1)
    tile_row = lax.broadcasted_iota(jnp.int32, (TILE, WIDTH), 0)
    value_extra = jnp.where(tile_lane < 3, -1.0, 0.0).astype(BF16)
    norm_extra = jnp.zeros((TILE, WIDTH), F32)
    for i, part in enumerate(ROOT_PARTS):
        norm_extra = jnp.where(tile_lane == BLOCK + i, -part, norm_extra)

    for half in range(2):
        here = slice(half * BLOCK, (half + 1) * BLOCK)
        for h in range(8):
            cols = slice(h * WIDTH, (h + 1) * WIDTH)
            there = slice(h * BLOCK, (h + 1) * BLOCK)
            g = g_ref[here, cols]
            q_all[half, there, :WIDTH] = q_ref[here, cols]
            g_all[half, there, :WIDTH] = g
            norm = norm_ref[here, h : h + 1].astype(F32)
            q_all[half, there, WIDTH:] = jnp.where(norm_lane, norm, one_hot).astype(BF16)
            delta = jnp.sum(g.astype(F32) * o_ref[here, cols].astype(F32), axis=1, keepdims=True)
            high = delta.astype(BF16).astype(F32)
            mid = (delta - high).astype(BF16).astype(F32)
            low = delta - high - mid
            extra = jnp.where(
                lane == 0, high, jnp.where(lane == 1, mid, jnp.where(lane == 2, low, 0.0))
            )
            g_all[half, there, WIDTH:] = extra.astype(BF16)
        q_turn[half] = q_all[half].T
        g_turn[half] = g_all[half].T

        p = order_ref[2 * span_ref[0] + half]
        first = p * BLOCK
        first_doc = jnp.int32(0)
        for s in starts:
            first_doc = jnp.maximum(first_doc, jnp.where(s <= first, s, 0))
        query_pos = tile_lane + first
        query_start = jnp.zeros_like(query_pos)
        for s in starts:
            query_start = jnp.maximum(query_start, jnp.where(s <= query_pos, s, 0))
        dq_turn[...] = jnp.zeros_like(dq_turn)

        def visit(t, carry):
            at = pl.multiple_of(t * TILE, TILE)
            tile = pl.ds(at, TILE)
            keys = k_pos[tile, :]
            key_pos = tile_row + at
            hidden = ((key_pos > query_pos) | (key_pos < query_start)) & (tile_lane < BLOCK)
            extra = jnp.where(hidden, MASKED, norm_extra).astype(BF16)
            scores = jnp.dot(
                jnp.concatenate([keys, extra], axis=1), q_turn[half],
                preferred_element_type=F32,
            )
            weights = jnp.exp2(scores * EXP2_SCALE)
            grad_weights = jnp.dot(
                jnp.concatenate([v_pos[tile, :], value_extra], axis=1), g_turn[half],
                preferred_element_type=F32,
            )
            grad_scores = (weights * grad_weights).astype(BF16)
            dv_acc[tile, :] += jnp.dot(
                weights.astype(BF16), g_all[half, :, :WIDTH], preferred_element_type=F32
            )
            dk_acc[tile, :] += jnp.dot(
                grad_scores, q_all[half, :, :WIDTH], preferred_element_type=F32
            )
            dq_turn[...] += jnp.dot(keys.T, grad_scores, preferred_element_type=F32)
            return carry

        lax.fori_loop(first_doc // TILE, first // TILE + 1, visit, 0)
        dq = (dq_turn[...] * SCALE).T
        for h in range(8):
            dq_ref[here, h * WIDTH : (h + 1) * WIDTH] = dq[h * BLOCK : (h + 1) * BLOCK].astype(BF16)

    def store_block(i, carry):
        at = pl.multiple_of(order_ref[i] * BLOCK, BLOCK)
        half = pl.multiple_of((i % 2) * BLOCK, BLOCK)
        dkv_ref[i // 2, 0, pl.ds(half, BLOCK), :] = (
            dk_acc[pl.ds(at, BLOCK), :] * SCALE
        ).astype(dkv_ref.dtype)
        dkv_ref[i // 2, 1, pl.ds(half, BLOCK), :] = dv_acc[pl.ds(at, BLOCK), :].astype(
            dkv_ref.dtype
        )
        return carry

    lax.fori_loop(0, blocks, store_block, 0, unroll=4)


def attend(span, order, docs, queries, output, grad_out, log_norm, kv, grad_dtype):
    spans, _, span_rows, _ = kv.shape
    length = spans * span_rows
    smem = pl.BlockSpec(memory_space=pltpu.SMEM)
    vmem = pl.BlockSpec(memory_space=pltpu.VMEM)
    return pl.pallas_call(
        attend_kernel,
        out_shape=(
            jax.ShapeDtypeStruct(queries.shape, BF16),
            jax.ShapeDtypeStruct(kv.shape, grad_dtype),
        ),
        in_specs=[smem, smem] + [vmem] * 6,
        out_specs=(vmem, vmem),
        scratch_shapes=[
            pltpu.VMEM((length, WIDTH), BF16),
            pltpu.VMEM((length, WIDTH), BF16),
            pltpu.VMEM((length, WIDTH), F32),
            pltpu.VMEM((length, WIDTH), F32),
            pltpu.VMEM((2, 8 * BLOCK, 2 * WIDTH), BF16),
            pltpu.VMEM((2, 8 * BLOCK, 2 * WIDTH), BF16),
            pltpu.VMEM((2, 2 * WIDTH, 8 * BLOCK), BF16),
            pltpu.VMEM((2, 2 * WIDTH, 8 * BLOCK), BF16),
            pltpu.VMEM((WIDTH, 8 * BLOCK), F32),
        ],
        compiler_params=pltpu.CompilerParams(vmem_limit_bytes=48 * 2**20),
        name="attend",
    )(span, order, docs, queries, output, grad_out, log_norm, kv)


def body(queries, key_matrix, value_matrix, output, grad_out, log_norm, doc_ids, block_order):
    span = lax.axis_index("blk").astype(jnp.int32).reshape(1)
    both = jnp.stack([key_matrix, value_matrix])
    rows_here = lax.all_to_all(both, "head", split_axis=2, concat_axis=1, tiled=True)
    kv = lax.all_gather(rows_here, "blk", axis=0, tiled=False)
    grad_query, grad_kv = attend(
        span, block_order, doc_ids.reshape(-1, WIDTH), queries, output, grad_out, log_norm, kv, F32
    )
    grad_here = lax.psum_scatter(grad_kv, "blk", scatter_dimension=0, tiled=False).astype(BF16)
    back = lax.all_to_all(grad_here, "head", split_axis=1, concat_axis=2, tiled=True)
    return (grad_query, back[0], back[1])


def solution(mesh):
    placed = (
        P("blk", "head"),
        P(("blk", "head"), None),
        P(("blk", "head"), None),
        P("blk", "head"),
        P("blk", "head"),
        P("blk", "head"),
        P(),
        P(),
    )
    return jax.shard_map(
        body,
        mesh=mesh,
        in_specs=placed,
        out_specs=(P("blk", "head"), P(("blk", "head"), None), P(("blk", "head"), None)),
        check_vma=False,
    )
```

time: 423 us -> 280 us (0.66)
  loops' own time: 44.2 us -> 0 us
  starting transfers between devices: 40.3 us -> 0.08 us
  waiting for transfers between devices: 249 us -> 210 us
  matrix products: 38.2 us -> 0 us
  blocking collectives: 0 us -> 36 us
  local copies, waits for them, and re-layouts: 37.5 us -> 9.7 us
  between operations: 2.02 us -> 14.1 us
  other arithmetic: 9.58 us -> 1.7 us
  Pallas kernels: 0 us -> 7.4 us
    ppermute x128 -> x0, waiting for transfers between devices: 224 us -> none  [shifted(): lax.ppermute(array, axis, [(i, (i + by) % length) for i in range(length)])]
    reduce_scatter x0 -> x1, waiting for transfers between devices: none -> 154 us  [body(): lax.psum_scatter(grad_kv, 'blk', scatter_dimension=0, tiled=False)]
    all_gather x0 -> x1, waiting for transfers between devices: none -> 56.1 us  [body(): kv = lax.all_gather(rows_here, 'blk', axis=0, tiled=False)]
    another operation x1 -> x0, loops' own time: 44.2 us -> none  [body(): final_state = lax.fori_loop(0, cycle_size // 2, two_turns, start_state)]
    dot_general x160 -> x0, matrix products: 38.2 us -> none  [the longest x32 8.32 us: tile_grads(): jnp.einsum('hgqk,khd->qhgd', scores_b, key_block, preferred_element_type=...]
    all_to_all x0 -> x2, blocking collectives: none -> 36 us  [the longest x1 20.1 us: body(): lax.all_to_all(both, 'head', split_axis=2, concat_axis=1, tiled=True)]
    all_to_all x4 -> x0, starting transfers between devices: 30.2 us -> none  [the longest x1 11.7 us: body(): lax.all_to_all(key_matrix, 'head', split_axis=1, concat_axis=0, tiled=True)]
    all_to_all x4 -> x0, waiting for transfers between devices: 24.4 us -> none  [the longest x1 8.63 us: body(): lax.all_to_all(value_matrix, 'head', split_axis=1, concat_axis=0, tiled=T...]
  transfers between devices with their start and end apart: 132 -> 2, of which waited for: 115 -> 2; matrix products, arithmetic and copies ran while one was open for 19% -> 0% of each run, Pallas kernels for 0% -> 0%
where the time goes in v1:
time: 280 us; the launch traced here: 279 us
  waiting for transfers between devices  210 us (75%)
  blocking collectives  36 us (13%)
  between operations  14.1 us (5%)
  local copies, waits for them, and re-layouts  9.7 us (3%)
  Pallas kernels  7.4 us (3%)
    reduce_scatter x1, waiting for transfers between devices, body(): lax.psum_scatter(grad_kv, 'blk', scatter_dimension=0, tiled=False)  154 us
    all_gather x1, waiting for transfers between devices, body(): kv = lax.all_gather(rows_here, 'blk', axis=0, tiled=False)  56.1 us
    all_to_all x1, blocking collectives, body(): lax.all_to_all(both, 'head', split_axis=2, concat_axis=1, tiled=True)  20.1 us
    all_to_all x1, blocking collectives, body(): lax.all_to_all(grad_here, 'head', split_axis=1, concat_axis=2, tiled=True)  15.9 us
    unnamed x15, local copies, waits for them, and re-layouts  7.53 us
    pallas_call x1, Pallas kernels, attend(): pl.pallas_call(attend_kernel, out_shape=(jax.ShapeDtypeStruct(queries.sha...  7.4 us
  transfers between devices with their start and end apart: 2, of which 2 were waited for; matrix products, arithmetic and copies ran while one was open for 0% of the time, Pallas kernels for 0%

profile of v1, /device:TPU:8, one launch (start us, length us, event | category | flops | bytes accessed | tf_op | source)
XLA Modules:
  0.0 279.3 jit_solution(17198231653852688365)
XLA Ops:
  7.2 0.0 all-gather.2.cloned.1.call-start
  7.2 0.8 pad_maximum_fusion
  8.0 0.4 copy.22
  8.4 0.5 reshape.20
  8.9 20.1 %all_to_all.30 = bf16[8,2,2048]{2,1,0:T(2,128)(2,1)S(1)} all-to-all(bf16[8,2,2048]{2,1,0:T(2,128)(2,1)S(1)} %reshape.20), channel_id=1, replica_groups=mesh['blk'=32,'head'=8] {'head'}, dimensions={0} | all-to-all | bytes 131072 | tf_op jit(solution)/shard_map/all_to_all | solution.py:183
  29.1 0.4 reshape.21
  29.4 1.0 copy.23
  30.4 0.0 all-gather.2.cloned.1.call-update
  30.4 0.0 reduce-scatter.2.cloned.1.call-start
  30.5 0.8 copy.24.norm_ref
  31.3 56.1 %all-gather.2.cloned.1.call-done.kv_ref = bf16[32,2,128,128]{3,2,1,0:T(8,128)(2,1)} async-done(((bf16[1,2,128,128]{3,2,1,0:T(8,128)(2,1)}), bf16[32,2,128,128]{3,2,1,0:T(8,128)(2,1)}) %all-gather.2.cloned.1.call-update) | async-done | bytes 2097168 | tf_op jit(solution)/shard_map/all_gather | solution.py:184
  87.4 0.0 copy-start
  87.4 1.6 copy-done
  89.0 0.0 copy-start.1
  89.0 0.9 copy-done.1
  89.9 0.0 copy-start.2
  89.9 0.9 copy-done.2
  90.9 0.0 copy-start.3
  90.9 0.9 copy-done.3
  91.8 0.0 copy-start.4
  91.8 0.7 copy-done.4
  92.5 0.0 copy-start.5
  92.5 0.7 copy-done.5
  93.2 7.4 %attend.1 = (bf16[128,1024]{1,0:T(8,128)(2,1)}, f32[32,2,128,128]{3,2,1,0:T(8,128)}) custom-call(s32[1]{0:T(128)} %bitcast.span_ref, s32[64]{0:T(128)S(1)} %copy-done.5, s32[32,128]{1,0:T(8,128)S(1)} %bitcast.23, bf16[128,1024]{1,0:T(8,128)(2,1)S(1)} %copy-done.1, bf16[128,1024]{1,0:T(8,128)(2,1)S(1)} %copy-done.2, bf16[128,1024]{1,0:T(8,128)(2,1)S(1)} %copy-done.3, ...), custom_call_target="tpu_custom_call" | custom-call | tf_op jit(solution)/shard_map/attend/pallas_call | solution.py:156
  100.6 0.0 reduce-scatter.2.cloned.1.call-update
  100.6 154.1 %reduce-scatter.2.cloned.1.call-done = f32[1,2,128,128]{3,2,1,0:T(8,128)} async-done(((f32[32,2,128,128]{3,2,1,0:T(8,128)}), f32[1,2,128,128]{3,2,1,0:T(8,128)}) %reduce-scatter.2.cloned.1.call-update) | async-done | bytes 131088 | tf_op jit(solution)/shard_map/reduce_scatter | solution.py:188
  254.7 0.9 convert_bitcast_fusion
  255.7 0.1 copy.25
  255.7 15.9 %all_to_all.31 = bf16[2,128,128]{2,0,1:T(2,128)(2,1)S(1)} all-to-all(bf16[2,128,128]{2,0,1:T(2,128)(2,1)S(1)} %copy.25), channel_id=1, replica_groups=mesh['blk'=32,'head'=8] {'head'}, dimensions={1} | all-to-all | bytes 131072 | tf_op jit(solution)/shard_map/all_to_all | solution.py:189
  271.6 0.1 fusion
  271.8 0.6 copy_bitcast_fusion
  (2 shorter events, 0.1 us)
Async XLA Ops:
  7.2 80.2 %all-gather.2.cloned.1.call-start = ((), (), s32[]{:S(2)}) async-start(), calls=%async_computation.3 | async-start | bytes 2162688 | tf_op jit(solution)/shard_map/all_gather | solution.py:184
  30.4 224.3 %reduce-scatter.2.cloned.1.call-start = ((), (), s32[]{:S(2)}) async-start(), calls=%async_computation.4 | async-start | bytes 4325376 | tf_op jit(solution)/shard_map/reduce_scatter | solution.py:188
  87.4 1.6 copy-start
  89.0 0.9 copy-start.1
  89.9 0.9 copy-start.2
  90.9 0.9 copy-start.3
  91.8 0.7 copy-start.4
  92.5 0.7 copy-start.5
Sparse Core Ops, SparseCore 0:
  30.5 56.7 all-gather.1
  100.7 153.9 reduce-scatter.1

commit v2 on v1

--- a/solution.py
+++ b/solution.py
@@ -177,17 +177,290 @@
     )(span, order, docs, queries, output, grad_out, log_norm, kv)
 
 
+class Place:
+    def __init__(self):
+        self.span = lax.axis_index("blk")
+        self.head = lax.axis_index("head")
+        self.core = self.span % 2
+        self.x = (self.span // 2) % 4
+        self.z = self.span // 8
+        self.near_z = (1 + self.z % 2, (2 + 3 * self.z) % 5, 3 * (1 - self.z // 2))
+
+    def at(self, z, dx=0, other=False):
+        core = 1 - self.core if other else self.core
+        return (z * 4 + (self.x + dx) % 4) * 2 + core
+
+    @property
+    def sibling(self):
+        return self.at(self.z, 0, True)
+
+
+def meet(place):
+    barrier = pltpu.get_barrier_semaphore()
+    peers = [(place.span, (place.head + d) % 8) for d in range(1, 8)]
+    peers += [(place.at(z), place.head) for z in place.near_z]
+    peers += [(place.at(place.z, 1), place.head), (place.at(place.z, 3), place.head)]
+    peers += [(place.sibling, place.head)]
+    for peer in peers:
+        pl.semaphore_signal(
+            barrier, inc=1, device_id=peer, device_id_type=pl.DeviceIdType.MESH
+        )
+    pl.semaphore_wait(barrier, len(peers))
+
+
+def copy_to(src, dst, send, recv, span, head):
+    return pltpu.make_async_remote_copy(
+        src_ref=src, dst_ref=dst, send_sem=send, recv_sem=recv,
+        device_id=(span, head), device_id_type=pl.DeviceIdType.MESH,
+    )
+
+
+def head_rows(head):
+    return pl.ds(pl.multiple_of(head * 16, 16), 16)
+
+
+def head_columns(head):
+    return pl.ds(pl.multiple_of(head * WIDTH, WIDTH), WIDTH)
+
+
+def gather_kernel(
+    k_ref, v_ref, kv_ref,
+    head_send, head_recv, z_send, z_recv, x_send, x_recv, f_send, f_recv, s_send, s_recv,
+):
+    me = Place()
+    own, head = me.span, me.head
+    meet(me)
+    sent = []
+
+    def send(*args):
+        copy = copy_to(*args)
+        copy.start()
+        sent.append(copy)
+
+    for d in range(1, 8):
+        peer = (head + d) % 8
+        for j, ref in enumerate((k_ref, v_ref)):
+            send(
+                ref.at[:, head_columns(peer)], kv_ref.at[own, j, head_rows(head), :],
+                head_send.at[j, d], head_recv.at[j, d], own, peer,
+            )
+    for j, ref in enumerate((k_ref, v_ref)):
+        kv_ref[own, j, head_rows(head), :] = ref[:, head_columns(head)]
+    for d in range(1, 8):
+        peer = (head + 8 - d) % 8
+        for j in range(2):
+            here = kv_ref.at[own, j, head_rows(peer), :]
+            copy_to(here, here, head_send.at[j, d], head_recv.at[j, d], own, peer).wait_recv()
+
+    order = (me.z,) + me.near_z
+    left, right, sibling = me.at(me.z, 3), me.at(me.z, 1), me.sibling
+
+    def arrived(part, recv, span):
+        copy_to(part, part, s_send.at[0, 0], recv, span, head).wait_recv()
+
+    def over(part, k, which):
+        send(part, part, s_send.at[k, which], s_recv.at[k, which], sibling, head)
+
+    def column(k):
+        span = me.at(order[k])
+        block = kv_ref.at[span]
+        if k > 0:
+            arrived(block, z_recv.at[order[k]], span)
+        send(block, block, x_send.at[0, k], x_recv.at[0, k], right, head)
+        send(block, block, x_send.at[1, k], x_recv.at[1, k], left, head)
+        if k == 0:
+            for i, z in enumerate(me.near_z):
+                send(block, block, z_send.at[i], z_recv.at[me.z], me.at(z), head)
+        over(block, k, 0)
+
+    def beside(k):
+        block = kv_ref.at[me.at(order[k], 3)]
+        arrived(block, x_recv.at[0, k], left)
+        send(block.at[0], block.at[0], f_send.at[0, k], f_recv.at[0, k], right, head)
+        over(block, k, 1)
+        block = kv_ref.at[me.at(order[k], 1)]
+        arrived(block, x_recv.at[1, k], right)
+        send(block.at[1], block.at[1], f_send.at[1, k], f_recv.at[1, k], left, head)
+        over(block, k, 2)
+
+    def across(k):
+        block = kv_ref.at[me.at(order[k], 2)]
+        arrived(block.at[0], f_recv.at[0, k], left)
+        over(block.at[0], k, 3)
+        arrived(block.at[1], f_recv.at[1, k], right)
+        over(block.at[1], k, 4)
+
+    column(0)
+    column(1)
+    beside(0)
+    column(2)
+    beside(1)
+    across(0)
+    column(3)
+    beside(2)
+    across(1)
+    beside(3)
+    across(2)
+    across(3)
+    for k in range(4):
+        for which, dx in enumerate((0, 3, 1)):
+            arrived(kv_ref.at[me.at(order[k], dx, True)], s_recv.at[k, which], sibling)
+        block = kv_ref.at[me.at(order[k], 2, True)]
+        arrived(block.at[0], s_recv.at[k, 3], sibling)
+        arrived(block.at[1], s_recv.at[k, 4], sibling)
+    for copy in sent:
+        copy.wait_send()
+
+
+def gather(key_matrix, value_matrix):
+    vmem = pl.BlockSpec(memory_space=pltpu.VMEM)
+    dma = pltpu.SemaphoreType.DMA
+    return pl.pallas_call(
+        gather_kernel,
+        out_shape=jax.ShapeDtypeStruct((32, 2, 2 * BLOCK, WIDTH), BF16),
+        in_specs=[vmem, vmem],
+        out_specs=vmem,
+        scratch_shapes=[
+            dma((2, 8)), dma((2, 8)), dma((3,)), dma((4,)), dma((2, 4)), dma((2, 4)),
+            dma((2, 4)), dma((2, 4)), dma((4, 5)), dma((4, 5)),
+        ],
+        compiler_params=pltpu.CompilerParams(
+            collective_id=0, has_side_effects=True, vmem_limit_bytes=32 * 2**20
+        ),
+        name="gather",
+    )(key_matrix, value_matrix)
+
+
+def scatter_kernel(
+    part_ref, dk_ref, dv_ref,
+    sib, far, near, deep, far_out, near_out, deep_out, total,
+    s_send, s_recv, f_send, f_recv, x_send, x_recv, z_send, z_recv, head_send, head_recv,
+):
+    me = Place()
+    own, head = me.span, me.head
+    meet(me)
+    sent = []
+
+    def send(*args):
+        copy = copy_to(*args)
+        copy.start()
+        sent.append(copy)
+
+    def arrived(part, recv, span):
+        copy_to(part, part, s_send.at[0, 0], recv, span, head).wait_recv()
+
+    order = me.near_z[::-1] + (me.z,)
+    left, right, sibling = me.at(me.z, 3), me.at(me.z, 1), me.sibling
+    for k in range(4):
+        for dx in (2, 1, 3, 0):
+            send(
+                part_ref.at[me.at(order[k], dx, True)], sib.at[k, dx],
+                s_send.at[k, dx], s_recv.at[k, dx], sibling, head,
+            )
+
+    def pair(k, dx, j):
+        return part_ref[me.at(order[k], dx), j].astype(F32) + sib[k, dx, j].astype(F32)
+
+    def across(k):
+        arrived(sib.at[k, 2], s_recv.at[k, 2], sibling)
+        for j, span in enumerate((right, left)):
+            far_out[k, j] = pair(k, 2, j).astype(BF16)
+            send(far_out.at[k, j], far.at[j, k], f_send.at[j, k], f_recv.at[j, k], span, head)
+
+    def beside(k):
+        for i, (dx, span, source) in enumerate(((1, right, left), (3, left, right))):
+            arrived(sib.at[k, dx], s_recv.at[k, dx], sibling)
+            arrived(far.at[i, k], f_recv.at[i, k], source)
+            near_out[i, k, i] = (pair(k, dx, i) + far[i, k].astype(F32)).astype(BF16)
+            near_out[i, k, 1 - i] = pair(k, dx, 1 - i).astype(BF16)
+            send(near_out.at[i, k], near.at[i, k], x_send.at[i, k], x_recv.at[i, k], span, head)
+
+    def column(k):
+        arrived(sib.at[k, 0], s_recv.at[k, 0], sibling)
+        arrived(near.at[0, k], x_recv.at[0, k], left)
+        arrived(near.at[1, k], x_recv.at[1, k], right)
+        sums = [
+            pair(k, 0, j) + near[0, k, j].astype(F32) + near[1, k, j].astype(F32)
+            for j in range(2)
+        ]
+        if k == 3:
+            return sums
+        for j in range(2):
+            deep_out[k, j] = sums[j].astype(BF16)
+        send(
+            deep_out.at[k], deep.at[me.z], z_send.at[k], z_recv.at[me.z], me.at(order[k]), head
+        )
+
+    for k in range(4):
+        across(k)
+    beside(0)
+    beside(1)
+    column(0)
+    beside(2)
+    column(1)
+    beside(3)
+    column(2)
+    sums = column(3)
+    for z in me.near_z:
+        arrived(deep.at[z], z_recv.at[z], me.at(z))
+        sums = [sums[j] + deep[z, j].astype(F32) for j in range(2)]
+    for j in range(2):
+        total[j] = sums[j].astype(BF16)
+    outs = (dk_ref, dv_ref)
+    for d in range(1, 8):
+        peer = (head + d) % 8
+        for j in range(2):
+            send(
+                total.at[j, head_rows(peer), :], outs[j].at[:, head_columns(head)],
+                head_send.at[j, d], head_recv.at[j, d], own, peer,
+            )
+    for j in range(2):
+        outs[j][:, head_columns(head)] = total[j, head_rows(head), :]
+    for d in range(1, 8):
+        peer = (head + 8 - d) % 8
+        for j in range(2):
+            here = outs[j].at[:, head_columns(peer)]
+            copy_to(here, here, head_send.at[j, d], head_recv.at[j, d], own, peer).wait_recv()
+    for copy in sent:
+        copy.wait_send()
+
+
+def scatter(parts):
+    vmem = pl.BlockSpec(memory_space=pltpu.VMEM)
+    dma = pltpu.SemaphoreType.DMA
+    chunk = (2 * BLOCK, WIDTH)
+    out = jax.ShapeDtypeStruct((16, 8 * WIDTH), BF16)
+    return pl.pallas_call(
+        scatter_kernel,
+        out_shape=(out, out),
+        in_specs=[vmem],
+        out_specs=(vmem, vmem),
+        scratch_shapes=[
+            pltpu.VMEM((4, 4, 2) + chunk, BF16),
+            pltpu.VMEM((2, 4) + chunk, BF16),
+            pltpu.VMEM((2, 4, 2) + chunk, BF16),
+            pltpu.VMEM((4, 2) + chunk, BF16),
+            pltpu.VMEM((4, 2) + chunk, BF16),
+            pltpu.VMEM((2, 4, 2) + chunk, BF16),
+            pltpu.VMEM((3, 2) + chunk, BF16),
+            pltpu.VMEM((2,) + chunk, BF16),
+            dma((4, 4)), dma((4, 4)), dma((2, 4)), dma((2, 4)), dma((2, 4)), dma((2, 4)),
+            dma((3,)), dma((4,)), dma((2, 8)), dma((2, 8)),
+        ],
+        compiler_params=pltpu.CompilerParams(
+            collective_id=1, has_side_effects=True, vmem_limit_bytes=32 * 2**20
+        ),
+        name="scatter",
+    )(parts)
+
+
 def body(queries, key_matrix, value_matrix, output, grad_out, log_norm, doc_ids, block_order):
     span = lax.axis_index("blk").astype(jnp.int32).reshape(1)
-    both = jnp.stack([key_matrix, value_matrix])
-    rows_here = lax.all_to_all(both, "head", split_axis=2, concat_axis=1, tiled=True)
-    kv = lax.all_gather(rows_here, "blk", axis=0, tiled=False)
+    kv = gather(key_matrix, value_matrix)
     grad_query, grad_kv = attend(
-        span, block_order, doc_ids.reshape(-1, WIDTH), queries, output, grad_out, log_norm, kv, F32
+        span, block_order, doc_ids.reshape(-1, WIDTH), queries, output, grad_out, log_norm, kv, BF16
     )
-    grad_here = lax.psum_scatter(grad_kv, "blk", scatter_dimension=0, tiled=False).astype(BF16)
-    back = lax.all_to_all(grad_here, "head", split_axis=1, concat_axis=2, tiled=True)
-    return (grad_query, back[0], back[1])
+    return (grad_query,) + tuple(scatter(grad_kv))
 
 
 def solution(mesh):

time: 280 us -> 74.5 us (0.27)
  the two profiles are of different devices: /device:TPU:8 before, /device:TPU:64 now
where the time goes in v2:
time: 74.5 us; the launch traced here: 74.3 us
  Pallas kernels  69.9 us (94%)
  local copies, waits for them, and re-layouts  3.63 us (5%)
    pallas_call x1, Pallas kernels, scatter(): pl.pallas_call(scatter_kernel, out_shape=(out, out), in_specs=[vmem], out...  34.4 us
    pallas_call x1, Pallas kernels, gather(): pl.pallas_call(gather_kernel, out_shape=jax.ShapeDtypeStruct((32, 2, 2 *...  30 us
    pallas_call x1, Pallas kernels, attend(): pl.pallas_call(attend_kernel, out_shape=(jax.ShapeDtypeStruct(queries.sha...  5.5 us
    unnamed x17, local copies, waits for them, and re-layouts  3.63 us

profile of v2, /device:TPU:64, one launch (start us, length us, event | category | flops | bytes accessed | tf_op | source)
XLA Modules:
  0.0 74.3 jit_solution(10380214122847332119)
XLA Ops:
  0.6 0.0 copy-start.2
  0.6 0.0 copy-start.1
  0.7 0.0 copy-start
  0.7 0.9 %copy.11.norm_ref = bf16[128,8]{1,0:T(8,128)(2,1)S(1)} copy(bf16[128,8]{0,1:T(8,128)(2,1)} %param.13) | data formatting | bytes 4096 | tf_op args[5]
  1.5 0.0 copy-start.3
  1.5 0.8 %copy-done.3 = bf16[16,1024]{1,0:T(8,128)(2,1)S(1)} copy-done((bf16[16,1024]{1,0:T(8,128)(2,1)S(1)}, bf16[16,1024]{1,0:T(8,128)(2,1)}, u32[]{:S(2)}) %copy-start.3) | copy-done | bytes 32792
  2.3 0.0 copy-start.4
  2.3 0.8 %copy-done.4 = bf16[16,1024]{1,0:T(8,128)(2,1)S(1)} copy-done((bf16[16,1024]{1,0:T(8,128)(2,1)S(1)}, bf16[16,1024]{1,0:T(8,128)(2,1)}, u32[]{:S(2)}) %copy-start.4) | copy-done | bytes 32792
  3.1 0.0 copy-start.5
  3.1 0.0 copy-start.6
  3.1 30.0 %gather.1.kv_ref = bf16[32,2,128,128]{3,2,1,0:T(8,128)(2,1)S(1)} custom-call(bf16[16,1024]{1,0:T(8,128)(2,1)S(1)} %copy-done.3, bf16[16,1024]{1,0:T(8,128)(2,1)S(1)} %copy-done.4), custom_call_target="tpu_custom_call" | custom-call | tf_op jit(solution)/shard_map/gather/pallas_call | solution.py:318
  33.1 0.0 copy-done.2
  33.1 0.0 copy-done.1
  33.1 0.0 copy-done
  33.1 0.0 copy-done.5
  33.1 0.0 copy-done.6
  33.2 5.5 %attend.1 = (bf16[128,1024]{1,0:T(8,128)(2,1)}, bf16[32,2,128,128]{3,2,1,0:T(8,128)(2,1)S(1)}) custom-call(s32[1]{0:T(128)} %bitcast.span_ref, s32[64]{0:T(128)S(1)} %copy-done.6, s32[32,128]{1,0:T(8,128)S(1)} %bitcast.2, bf16[128,1024]{1,0:T(8,128)(2,1)S(1)} %copy-done, bf16[128,1024]{1,0:T(8,128)(2,1)S(1)} %copy-done.1, bf16[128,1024]{1,0:T(8,128)(2,1)S(1)} %copy-done.2, ...), custom_call_target="tpu_custom_call" | custom-call | tf_op jit(solution)/shard_map/attend/pallas_call | solution.py:156
  38.7 34.4 %scatter.1 = (bf16[16,1024]{1,0:T(8,128)(2,1)S(1)}, bf16[16,1024]{1,0:T(8,128)(2,1)S(1)}) custom-call(bf16[32,2,128,128]{3,2,1,0:T(8,128)(2,1)S(1)} %get-tuple-element.8.part_ref), custom_call_target="tpu_custom_call" | custom-call | tf_op jit(solution)/shard_map/scatter/pallas_call | solution.py:433
  73.0 0.6 copy.14
  73.7 0.6 copy.15
Async XLA Ops:
  0.6 32.5 %copy-start.2 = (bf16[128,1024]{1,0:T(8,128)(2,1)S(1)}, bf16[128,1024]{1,0:T(8,128)(2,1)}, u32[]{:S(2)}) copy-start(bf16[128,1024]{1,0:T(8,128)(2,1)} %g_ref.1) | copy-start | bytes 786436
  0.6 32.5 %copy-start.1 = (bf16[128,1024]{1,0:T(8,128)(2,1)S(1)}, bf16[128,1024]{1,0:T(8,128)(2,1)}, u32[]{:S(2)}) copy-start(bf16[128,1024]{1,0:T(8,128)(2,1)} %o_ref.1) | copy-start | bytes 786436
  0.7 32.5 %copy-start = (bf16[128,1024]{1,0:T(8,128)(2,1)S(1)}, bf16[128,1024]{1,0:T(8,128)(2,1)}, u32[]{:S(2)}) copy-start(bf16[128,1024]{1,0:T(8,128)(2,1)} %q_ref.1) | copy-start | bytes 786436
  1.5 0.8 %copy-start.3 = (bf16[16,1024]{1,0:T(8,128)(2,1)S(1)}, bf16[16,1024]{1,0:T(8,128)(2,1)}, u32[]{:S(2)}) copy-start(bf16[16,1024]{1,0:T(8,128)(2,1)} %k_ref.1) | copy-start | bytes 98308
  2.3 0.8 %copy-start.4 = (bf16[16,1024]{1,0:T(8,128)(2,1)S(1)}, bf16[16,1024]{1,0:T(8,128)(2,1)}, u32[]{:S(2)}) copy-start(bf16[16,1024]{1,0:T(8,128)(2,1)} %v_ref.1) | copy-start | bytes 98308
  3.1 30.1 %copy-start.5 = (s32[4096]{0:T(1024)S(1)}, s32[4096]{0:T(1024)}, u32[]{:S(2)}) copy-start(s32[4096]{0:T(1024)} %param.14) | copy-start | bytes 49156
  3.1 30.1 %copy-start.6 = (s32[64]{0:T(128)S(1)}, s32[64]{0:T(128)}, u32[]{:S(2)}) copy-start(s32[64]{0:T(128)} %order_ref.1) | copy-start | bytes 772

commit v3 on v1

v3 whole, which is shorter than its diff:
```python
import functools
import math

import jax
import jax.numpy as jnp
from jax import lax
from jax.experimental import pallas as pl
from jax.experimental.pallas import tpu as pltpu
from jax.sharding import PartitionSpec as P

WIDTH = 128
BLOCK = 64
DOCS = 6
TILE = 256
MASKED = -(2.0**17)
ROOT = math.sqrt(WIDTH)
SCALE = 1.0 / ROOT
EXP2_SCALE = SCALE * math.log2(math.e)
BF16 = jnp.bfloat16
F32 = jnp.float32


def root_parts():
    parts, rest = [], ROOT
    for _ in range(3):
        term = _to_bf16(rest)
        parts.append(term)
        rest -= term
    return parts


def _to_bf16(value):
    mantissa, exponent = math.frexp(value)
    return math.ldexp(round(mantissa * 256), exponent - 8)


ROOT_PARTS = root_parts()


class Place:
    def __init__(self):
        self.span = lax.axis_index("blk")
        self.head = lax.axis_index("head")
        self.core = self.span % 2
        self.x = (self.span // 2) % 4
        self.z = self.span // 8
        self.near_z = (1 + self.z % 2, (2 + 3 * self.z) % 5, 3 * (1 - self.z // 2))

    def at(self, z, dx=0, other=False):
        core = 1 - self.core if other else self.core
        return (z * 4 + (self.x + dx) % 4) * 2 + core

    @property
    def sibling(self):
        return self.at(self.z, 0, True)


def meet(place):
    barrier = pltpu.get_barrier_semaphore()
    peers = [(place.span, (place.head + d) % 8) for d in range(1, 8)]
    peers += [(place.at(z), place.head) for z in place.near_z]
    peers += [(place.at(place.z, 1), place.head), (place.at(place.z, 3), place.head)]
    peers += [(place.sibling, place.head)]
    for peer in peers:
        pl.semaphore_signal(
            barrier, inc=1, device_id=peer, device_id_type=pl.DeviceIdType.MESH
        )
    pl.semaphore_wait(barrier, len(peers))


class Sent:
    def __init__(self, ref):
        self.ref = ref

    @property
    def at(self):
        return self

    def __getitem__(self, index):
        return (self.ref, index)


def copy_to(src, dst, send, recv, span, head):
    ref, index = send
    send = ref.at[index]
    return pltpu.make_async_remote_copy(
        src_ref=src, dst_ref=dst, send_sem=send, recv_sem=recv,
        device_id=(span, head), device_id_type=pl.DeviceIdType.MESH,
    )


def head_rows(head):
    return pl.ds(pl.multiple_of(head * 16, 16), 16)


def head_columns(head):
    return pl.ds(pl.multiple_of(head * WIDTH, WIDTH), WIDTH)


OWN, LEFT, RIGHT, FAR = 0, 3, 1, 2
UNITS = [
    (0, OWN), (1, OWN), (0, LEFT), (0, RIGHT), (2, OWN), (0, FAR), (1, LEFT), (1, RIGHT),
    (3, OWN), (1, FAR), (2, LEFT), (2, RIGHT), (2, FAR), (3, LEFT), (3, RIGHT), (3, FAR),
]
STEP_OF = {unit: step for step, unit in enumerate(UNITS)}


def backward_kernel(
    order_ref, docs_hbm, q_hbm, o_hbm, g_hbm, norm_ref, k_hbm, v_hbm,
    dq_ref, dk_ref, dv_ref,
    docs_ref, q_ref, o_ref, g_ref, k_ref, v_ref,
    kv_ref, q_all, g_all, q_turn, g_turn, dq_turn, work,
    part, sib_out, sib, far, near, deep, far_out, near_out, deep_out, total,
    load_sem,
    head_send, head_recv, z_send, z_recv, x_send, x_recv, f_send, f_recv, s_send, s_recv,
    p_send, p_recv, rf_send, rf_recv, rx_send, rx_recv, rz_send, rz_recv, rh_send, rh_recv,
):
    (
        head_send, z_send, x_send, f_send, s_send, p_send, rf_send, rx_send, rz_send, rh_send
    ) = map(
        Sent,
        (head_send, z_send, x_send, f_send, s_send, p_send, rf_send, rx_send, rz_send, rh_send),
    )
    me = Place()
    own, head = me.span, me.head
    order = (me.z,) + me.near_z
    left, right, sibling = me.at(me.z, LEFT), me.at(me.z, RIGHT), me.sibling

    loads = [
        pltpu.make_async_copy(src, dst, load_sem.at[i])
        for i, (src, dst) in enumerate(
            (
                (k_hbm, k_ref), (v_hbm, v_ref), (q_hbm, q_ref), (g_hbm, g_ref),
                (o_hbm, o_ref), (docs_hbm, docs_ref),
            )
        )
    ]
    for load in loads:
        load.start()
    meet(me)
    loads[0].wait()
    loads[1].wait()

    sent = []

    def send(src, dst, sent_sem, recv_sem, span, to_head):
        copy_to(src, dst, sent_sem, recv_sem, span, to_head).start()
        sent.append((src.shape, sent_sem))

    def arrived(block, recv, span):
        copy_to(block, block, s_send.at[0, 0], recv, span, head).wait_recv()

    for d in range(1, 8):
        peer = (head + d) % 8
        for j, ref in enumerate((k_ref, v_ref)):
            send(
                ref.at[:, head_columns(peer)], kv_ref.at[own, j, head_rows(head), :],
                head_send.at[j, d], head_recv.at[j, d], own, peer,
            )
    for j, ref in enumerate((k_ref, v_ref)):
        kv_ref[own, j, head_rows(head), :] = ref[:, head_columns(head)]

    for load in loads[2:]:
        load.wait()
    docs = docs_ref[...]
    starts = [jnp.sum((docs < d).astype(jnp.int32)) for d in range(1, DOCS)]
    lane = lax.broadcasted_iota(jnp.int32, (BLOCK, WIDTH), 1)
    row = lax.broadcasted_iota(jnp.int32, (BLOCK, WIDTH), 0)
    one_hot = (lane == row).astype(F32)
    norm_lane = (lane >= BLOCK) & (lane < BLOCK + 3)
    lanes = lax.broadcasted_iota(jnp.int32, (1, WIDTH), 1)
    norms = norm_ref[...].astype(F32).T
    query_pos, query_start = [], []
    for half in range(2):
        here = slice(half * BLOCK, (half + 1) * BLOCK)
        for h in range(8):
            cols = slice(h * WIDTH, (h + 1) * WIDTH)
            there = slice(h * BLOCK, (h + 1) * BLOCK)
            g = g_ref[here, cols]
            q_all[half, there, :WIDTH] = q_ref[here, cols]
            g_all[half, there, :WIDTH] = g
            norm = norms[here, h : h + 1]
            q_all[half, there, WIDTH:] = jnp.where(norm_lane, norm, one_hot).astype(BF16)
            delta = jnp.sum(g.astype(F32) * o_ref[here, cols].astype(F32), axis=1, keepdims=True)
            high = delta.astype(BF16).astype(F32)
            mid = (delta - high).astype(BF16).astype(F32)
            low = delta - high - mid
            extra = jnp.where(
                lane == 0, high, jnp.where(lane == 1, mid, jnp.where(lane == 2, low, 0.0))
            )
            g_all[half, there, WIDTH:] = extra.astype(BF16)
        q_turn[half] = q_all[half].T
        g_turn[half] = g_all[half].T
        dq_turn[half] = jnp.zeros((WIDTH, 8 * BLOCK), F32)
        pos = lanes + order_ref[2 * own + half] * BLOCK
        start = jnp.zeros_like(pos)
        for s in starts:
            start = jnp.maximum(start, jnp.where(s <= pos, s, 0))
        query_pos.append(jnp.where(lanes < BLOCK, pos, 1 << 20))
        query_start.append(jnp.where(lanes < BLOCK, start, 0))
    tile_lane = lax.broadcasted_iota(jnp.int32, (TILE, WIDTH), 1)
    value_extra = jnp.where(tile_lane < 3, -1.0, 0.0).astype(BF16)
    norm_extra = jnp.zeros((1, WIDTH), F32)
    for i, term in enumerate(ROOT_PARTS):
        norm_extra = jnp.where(lanes == BLOCK + i, -term, norm_extra)

    for d in range(1, 8):
        peer = (head + 8 - d) % 8
        for j in range(2):
            here = kv_ref.at[own, j, head_rows(peer), :]
            copy_to(here, here, head_send.at[j, d], head_recv.at[j, d], own, peer).wait_recv()

    def over(block, k, which):
        send(block, block, s_send.at[k, which], s_recv.at[k, which], sibling, head)

    def give_column(k):
        span = me.at(order[k])
        block = kv_ref.at[span]
        if k > 0:
            arrived(block, z_recv.at[order[k]], span)
        send(block, block, x_send.at[0, k], x_recv.at[0, k], right, head)
        send(block, block, x_send.at[1, k], x_recv.at[1, k], left, head)
        if k == 0:
            for i, z in enumerate(me.near_z):
                send(block, block, z_send.at[i], z_recv.at[me.z], me.at(z), head)
        over(block, k, 0)

    def give_beside(k):
        block = kv_ref.at[me.at(order[k], LEFT)]
        arrived(block, x_recv.at[0, k], left)
        send(block.at[0], block.at[0], f_send.at[0, k], f_recv.at[0, k], right, head)
        over(block, k, 1)
        block = kv_ref.at[me.at(order[k], RIGHT)]
        arrived(block, x_recv.at[1, k], right)
        send(block.at[1], block.at[1], f_send.at[1, k], f_recv.at[1, k], left, head)
        over(block, k, 2)

    def give_far(k):
        block = kv_ref.at[me.at(order[k], FAR)]
        arrived(block.at[0], f_recv.at[0, k], left)
        over(block.at[0], k, 3)
        arrived(block.at[1], f_recv.at[1, k], right)
        over(block.at[1], k, 4)

    def ready(k, dx):
        block = kv_ref.at[me.at(order[k], dx, True)]
        if dx == FAR:
            arrived(block.at[0], s_recv.at[k, 3], sibling)
            arrived(block.at[1], s_recv.at[k, 4], sibling)
        else:
            arrived(block, s_recv.at[k, {OWN: 0, LEFT: 1, RIGHT: 2}[dx]], sibling)

    def pair(k, dx, j):
        step = STEP_OF[k, dx]
        return part[step, j] + sib[step, j].astype(F32)

    def met(k, dx):
        step = STEP_OF[k, dx]
        arrived(sib.at[step], p_recv.at[step], sibling)

    def sum_far(k):
        met(k, FAR)
        for j, span in enumerate((right, left)):
            far_out[k, j] = pair(k, FAR, j).astype(BF16)
            send(far_out.at[k, j], far.at[j, k], rf_send.at[j, k], rf_recv.at[j, k], span, head)

    def sum_beside(k):
        for i, (dx, span, source) in enumerate(((RIGHT, right, left), (LEFT, left, right))):
            met(k, dx)
            arrived(far.at[i, k], rf_recv.at[i, k], source)
            near_out[i, k, i] = (pair(k, dx, i) + far[i, k].astype(F32)).astype(BF16)
            near_out[i, k, 1 - i] = pair(k, dx, 1 - i).astype(BF16)
            send(
                near_out.at[i, k], near.at[i, k], rx_send.at[i, k], rx_recv.at[i, k], span, head
            )

    def sum_column(k):
        met(k, OWN)
        arrived(near.at[0, k], rx_recv.at[0, k], left)
        arrived(near.at[1, k], rx_recv.at[1, k], right)
        sums = [
            pair(k, OWN, j) + near[0, k, j].astype(F32) + near[1, k, j].astype(F32)
            for j in range(2)
        ]
        if k == 0:
            return sums
        for j in range(2):
            deep_out[k, j] = sums[j].astype(BF16)
        send(
            deep_out.at[k], deep.at[me.z], rz_send.at[k], rz_recv.at[me.z], me.at(order[k]), head
        )

    before = {
        0: [(give_column, 0)],
        1: [(give_beside, 0), (give_column, 1)],
        2: [(give_column, 2)],
        3: [(give_far, 0)],
        4: [(give_beside, 1), (give_column, 3)],
        6: [(give_beside, 2), (give_far, 1)],
        8: [(give_beside, 3), (give_far, 2)],
        9: [(sum_far, 0)],
        11: [(give_far, 3)],
        13: [(sum_far, 1), (sum_beside, 0)],
        15: [(sum_far, 2)],
    }
    chips = [order[k] * 4 + (me.x + dx) % 4 for k, dx in UNITS]
    block_row = lax.broadcasted_iota(jnp.int32, (BLOCK, WIDTH), 0)

    def unit(step, carry):
        for at, (k, dx) in enumerate(UNITS):

            @pl.when(step == at)
            def _():
                for action, which in before.get(at, []):
                    action(which)
                ready(k, dx)

        chip = chips[0]
        for at in range(1, len(UNITS)):
            chip = jnp.where(step == at, chips[at], chip)
        keys = kv_ref[pl.ds(2 * chip, 2), 0].reshape(TILE, WIDTH)
        values = kv_ref[pl.ds(2 * chip, 2), 1].reshape(TILE, WIDTH)
        key_pos = jnp.concatenate(
            [block_row + order_ref[4 * chip + i] * BLOCK for i in range(4)], axis=0
        )
        value_side = jnp.concatenate([values, value_extra], axis=1)
        keys_turn = keys.T
        grad_keys = grad_values = None
        for half in range(2):
            hidden = (key_pos > query_pos[half]) | (key_pos < query_start[half])
            extra = jnp.where(hidden, MASKED, norm_extra).astype(BF16)
            scores = jnp.dot(
                jnp.concatenate([keys, extra], axis=1), q_turn[half], preferred_element_type=F32
            )
            weights = jnp.exp2(scores * EXP2_SCALE)
            grad_weights = jnp.dot(value_side, g_turn[half], preferred_element_type=F32)
            grad_scores = (weights * grad_weights).astype(BF16)
            to_values = jnp.dot(
                weights.astype(BF16), g_all[half, :, :WIDTH], preferred_element_type=F32
            )
            to_keys = jnp.dot(grad_scores, q_all[half, :, :WIDTH], preferred_element_type=F32)
            dq_turn[half] += jnp.dot(keys_turn, grad_scores, preferred_element_type=F32)
            grad_keys = to_keys if half == 0 else grad_keys + to_keys
            grad_values = to_values if half == 0 else grad_values + to_values
        for i in range(2):
            rows = slice(2 * i * BLOCK, 2 * (i + 1) * BLOCK)
            work[i, 0] = grad_keys[rows] * SCALE
            work[i, 1] = grad_values[rows]
        part[step] = work[me.core]
        sib_out[step] = work[1 - me.core].astype(BF16)
        copy_to(
            sib_out.at[step], sib.at[step], p_send.at[step], p_recv.at[step], sibling, head
        ).start()
        return carry

    lax.fori_loop(0, len(UNITS), unit, 0)
    sum_beside(1)
    sum_far(3)
    for half in range(2):
        dq = (dq_turn[half] * SCALE).T
        for h in range(8):
            dq_ref[half * BLOCK : (half + 1) * BLOCK, h * WIDTH : (h + 1) * WIDTH] = dq[
                h * BLOCK : (h + 1) * BLOCK
            ].astype(BF16)
    sum_beside(2)
    sum_column(1)
    sum_beside(3)
    sum_column(2)
    sum_column(3)
    sums = sum_column(0)
    for z in me.near_z:
        arrived(deep.at[z], rz_recv.at[z], me.at(z))
        sums = [sums[j] + deep[z, j].astype(F32) for j in range(2)]
    for j in range(2):
        total[j] = sums[j].astype(BF16)
    outs = (dk_ref, dv_ref)
    for d in range(1, 8):
        peer = (head + d) % 8
        for j in range(2):
            send(
                total.at[j, head_rows(peer), :], outs[j].at[:, head_columns(head)],
                rh_send.at[j, d], rh_recv.at[j, d], own, peer,
            )
    for j in range(2):
        outs[j][:, head_columns(head)] = total[j, head_rows(head), :]
    for d in range(1, 8):
        peer = (head + 8 - d) % 8
        for j in range(2):
            here = outs[j].at[:, head_columns(peer)]
            copy_to(here, here, rh_send.at[j, d], rh_recv.at[j, d], own, peer).wait_recv()
    sent += [(sib_out.shape[1:], p_send.at[step]) for step in range(len(UNITS))]
    shapes = {
        (2, 2 * BLOCK, WIDTH): kv_ref.at[0],
        (2 * BLOCK, WIDTH): kv_ref.at[0, 0],
        (16, WIDTH): kv_ref.at[0, 0, pl.ds(0, 16), :],
    }
    for shape, sent_sem in sent:
        block = shapes[tuple(shape)]
        copy_to(block, block, sent_sem, s_recv.at[0, 0], sibling, head).wait_send()


def backward(order, docs, queries, output, grad_out, norm_turn, key_matrix, value_matrix):
    smem = pl.BlockSpec(memory_space=pltpu.SMEM)
    vmem = pl.BlockSpec(memory_space=pltpu.VMEM)
    hbm = pl.BlockSpec(memory_space=pl.ANY)
    dma = pltpu.SemaphoreType.DMA
    chunk = (2 * BLOCK, WIDTH)
    rows = 8 * BLOCK
    out = jax.ShapeDtypeStruct(key_matrix.shape, BF16)
    return pl.pallas_call(
        backward_kernel,
        out_shape=(jax.ShapeDtypeStruct(queries.shape, BF16), out, out),
        in_specs=[smem, hbm, hbm, hbm, hbm, vmem, hbm, hbm],
        out_specs=(vmem, vmem, vmem),
        scratch_shapes=[
            pltpu.VMEM(docs.shape, jnp.int32),
            pltpu.VMEM(queries.shape, BF16),
            pltpu.VMEM(queries.shape, BF16),
            pltpu.VMEM(queries.shape, BF16),
            pltpu.VMEM(key_matrix.shape, BF16),
            pltpu.VMEM(key_matrix.shape, BF16),
            pltpu.VMEM((32, 2) + chunk, BF16),
            pltpu.VMEM((2, rows, 2 * WIDTH), BF16),
            pltpu.VMEM((2, rows, 2 * WIDTH), BF16),
            pltpu.VMEM((2, 2 * WIDTH, rows), BF16),
            pltpu.VMEM((2, 2 * WIDTH, rows), BF16),
            pltpu.VMEM((2, WIDTH, rows), F32),
            pltpu.VMEM((2, 2) + chunk, F32),
            pltpu.VMEM((16, 2) + chunk, F32),
            pltpu.VMEM((16, 2) + chunk, BF16),
            pltpu.VMEM((16, 2) + chunk, BF16),
            pltpu.VMEM((2, 4) + chunk, BF16),
            pltpu.VMEM((2, 4, 2) + chunk, BF16),
            pltpu.VMEM((4, 2) + chunk, BF16),
            pltpu.VMEM((4, 2) + chunk, BF16),
            pltpu.VMEM((2, 4, 2) + chunk, BF16),
            pltpu.VMEM((4, 2) + chunk, BF16),
            pltpu.VMEM((2,) + chunk, BF16),
            dma((6,)),
            dma((2, 8)), dma((2, 8)), dma((3,)), dma((4,)), dma((2, 4)), dma((2, 4)),
            dma((2, 4)), dma((2, 4)), dma((4, 5)), dma((4, 5)),
            dma((16,)), dma((16,)), dma((2, 4)), dma((2, 4)), dma((2, 4)), dma((2, 4)),
            dma((4,)), dma((4,)), dma((2, 8)), dma((2, 8)),
        ],
        compiler_params=pltpu.CompilerParams(
            collective_id=0, has_side_effects=True, vmem_limit_bytes=56 * 2**20
        ),
        name="backward",
    )(order, docs, queries, output, grad_out, norm_turn, key_matrix, value_matrix)


def body(queries, key_matrix, value_matrix, output, grad_out, log_norm, doc_ids, block_order):
    return backward(
        block_order, doc_ids.reshape(-1, WIDTH), queries, output, grad_out, log_norm.T,
        key_matrix, value_matrix,
    )


def solution(mesh):
    placed = (
        P("blk", "head"),
        P(("blk", "head"), None),
        P(("blk", "head"), None),
        P("blk", "head"),
        P("blk", "head"),
        P("blk", "head"),
        P(),
        P(),
    )
    return jax.shard_map(
        body,
        mesh=mesh,
        in_specs=placed,
        out_specs=(P("blk", "head"), P(("blk", "head"), None), P(("blk", "head"), None)),
        check_vma=False,
    )
```

time: 280 us -> 69 us (0.25)
  waiting for transfers between devices: 210 us -> 0 us
  Pallas kernels: 7.4 us -> 64.7 us
  blocking collectives: 36 us -> 0 us
  between operations: 14.1 us -> 0.65 us
  local copies, waits for them, and re-layouts: 9.7 us -> 3.06 us
    reduce_scatter x1 -> x0, waiting for transfers between devices: 154 us -> none  [body(): lax.psum_scatter(grad_kv, 'blk', scatter_dimension=0, tiled=False)]
    pallas_call x1, Pallas kernels: 7.4 us -> 64.7 us  [backward(): pl.pallas_call(backward_kernel, out_shape=(jax.ShapeDtypeStruct(queries.s...]
    all_gather x1 -> x0, waiting for transfers between devices: 56.1 us -> none  [body(): kv = lax.all_gather(rows_here, 'blk', axis=0, tiled=False)]
    all_to_all x2 -> x0, blocking collectives: 36 us -> none  [the longest x1 20.1 us: body(): lax.all_to_all(both, 'head', split_axis=2, concat_axis=1, tiled=True)]
    unnamed x15 -> x7, local copies, waits for them, and re-layouts: 7.53 us -> 3.06 us
  transfers between devices with their start and end apart: 2 -> 0, of which waited for: 2 -> 0; matrix products, arithmetic and copies ran while one was open for 0% -> 0% of each run, Pallas kernels for 0% -> 0%
where the time goes in v3:
time: 69 us; the launch traced here: 68.5 us
  Pallas kernels  64.7 us (94%)
  local copies, waits for them, and re-layouts  3.06 us (4%)
    pallas_call x1, Pallas kernels, backward(): pl.pallas_call(backward_kernel, out_shape=(jax.ShapeDtypeStruct(queries.s...  64.7 us
    unnamed x7, local copies, waits for them, and re-layouts  3.06 us

profile of v3, /device:TPU:8, one launch (start us, length us, event | category | flops | bytes accessed | tf_op | source)
XLA Modules:
  0.0 68.5 jit_solution(16852241599719242617)
XLA Ops:
  0.6 64.7 %backward.1 = (bf16[128,1024]{1,0:T(8,128)(2,1)}, bf16[16,1024]{1,0:T(8,128)(2,1)}, bf16[16,1024]{1,0:T(8,128)(2,1)}) custom-call(s32[64]{0:T(128)} %order_ref.1, s32[32,128]{1,0:T(8,128)} %bitcast.2, bf16[128,1024]{1,0:T(8,128)(2,1)} %q_hbm.1, bf16[128,1024]{1,0:T(8,128)(2,1)} %o_hbm.1, bf16[128,1024]{1,0:T(8,128)(2,1)} %g_hbm.1, bf16[8,128]{1,0:T(8,128)(2,1)} %bitcast.3, ...), custom_call_target="tpu_custom_call" | custom-call | tf_op jit(solution)/shard_map/backward/pallas_call | solution.py:410
  65.4 0.0 copy-start.1
  65.4 1.7 %copy.14 = bf16[128,1024]{1,0:T(8,128)(2,1)} copy(bf16[128,1024]{1,0:T(8,128)(2,1)} %get-tuple-element.6) | data formatting | bytes 524288
  67.1 0.0 copy-done.1
  67.1 0.0 copy-start
  67.1 0.6 copy.15
  67.7 0.2 copy-done
  67.8 0.6 copy.16
Async XLA Ops:
  65.4 1.7 %copy-start.1 = (bf16[16,1024]{1,0:T(8,128)(2,1)S(1)}, bf16[16,1024]{1,0:T(8,128)(2,1)}, u32[]{:S(2)}) copy-start(bf16[16,1024]{1,0:T(8,128)(2,1)} %get-tuple-element.7) | copy-start | bytes 98308
  67.1 0.8 %copy-start = (bf16[16,1024]{1,0:T(8,128)(2,1)S(1)}, bf16[16,1024]{1,0:T(8,128)(2,1)}, u32[]{:S(2)}) copy-start(bf16[16,1024]{1,0:T(8,128)(2,1)} %get-tuple-element.8) | copy-start | bytes 98308

commit v4 on v3

--- a/solution.py
+++ b/solution.py
@@ -44,12 +44,17 @@
         self.core = self.span % 2
         self.x = (self.span // 2) % 4
         self.z = self.span // 8
+        self.high, self.y = self.head // 4, self.head % 4
+        self.partner = (1 - self.high) * 4 + self.y
         self.near_z = (1 + self.z % 2, (2 + 3 * self.z) % 5, 3 * (1 - self.z // 2))
 
     def at(self, z, dx=0, other=False):
         core = 1 - self.core if other else self.core
         return (z * 4 + (self.x + dx) % 4) * 2 + core
 
+    def beside_y(self, d):
+        return self.high * 4 + (self.y + d) % 4
+
     @property
     def sibling(self):
         return self.at(self.z, 0, True)
@@ -57,8 +62,9 @@
 
 def meet(place):
     barrier = pltpu.get_barrier_semaphore()
-    peers = [(place.span, (place.head + d) % 8) for d in range(1, 8)]
+    peers = [(place.span, place.beside_y(d)) for d in range(1, 4)]
     peers += [(place.at(z), place.head) for z in place.near_z]
+    peers += [(place.at(z), place.partner) for z in (place.z,) + place.near_z]
     peers += [(place.at(place.z, 1), place.head), (place.at(place.z, 3), place.head)]
     peers += [(place.sibling, place.head)]
     for peer in peers:
@@ -93,6 +99,10 @@
     return pl.ds(pl.multiple_of(head * 16, 16), 16)
 
 
+def half_rows(high):
+    return pl.ds(pl.multiple_of(high * BLOCK, BLOCK), BLOCK)
+
+
 def head_columns(head):
     return pl.ds(pl.multiple_of(head * WIDTH, WIDTH), WIDTH)
 
@@ -100,8 +110,10 @@
 OWN, LEFT, RIGHT, FAR = 0, 3, 1, 2
 UNITS = [
     (0, OWN), (1, OWN), (0, LEFT), (0, RIGHT), (2, OWN), (0, FAR), (1, LEFT), (1, RIGHT),
-    (3, OWN), (1, FAR), (2, LEFT), (2, RIGHT), (2, FAR), (3, LEFT), (3, RIGHT), (3, FAR),
+    (1, FAR), (2, LEFT), (2, RIGHT), (2, FAR), (3, FAR), (3, LEFT), (3, RIGHT), (3, OWN),
 ]
+ALL, MINE, OTHER = 0, 1, 2
+ITEMS = [(0, MINE), (1, ALL), (0, OTHER), (2, ALL), (3, ALL)]
 STEP_OF = {unit: step for step, unit in enumerate(UNITS)}
 
 
@@ -109,8 +121,8 @@
     order_ref, docs_hbm, q_hbm, o_hbm, g_hbm, norm_ref, k_hbm, v_hbm,
     dq_ref, dk_ref, dv_ref,
     docs_ref, q_ref, o_ref, g_ref, k_ref, v_ref,
-    kv_ref, q_all, g_all, q_turn, g_turn, dq_turn, work,
-    part, sib_out, sib, far, near, deep, far_out, near_out, deep_out, total,
+    kv_ref, other_ref, q_all, g_all, q_turn, g_turn, dq_turn, work,
+    part, sib_out, sib, far, near, deep, far_out, near_out, deep_out, total, deep_sum, mine_sum,
     load_sem,
     head_send, head_recv, z_send, z_recv, x_send, x_recv, f_send, f_recv, s_send, s_recv,
     p_send, p_recv, rf_send, rf_recv, rx_send, rx_recv, rz_send, rz_recv, rh_send, rh_recv,
@@ -150,15 +162,20 @@
     def arrived(block, recv, span):
         copy_to(block, block, s_send.at[0, 0], recv, span, head).wait_recv()
 
-    for d in range(1, 8):
-        peer = (head + d) % 8
-        for j, ref in enumerate((k_ref, v_ref)):
-            send(
-                ref.at[:, head_columns(peer)], kv_ref.at[own, j, head_rows(head), :],
-                head_send.at[j, d], head_recv.at[j, d], own, peer,
-            )
+    homes = (kv_ref.at[own, :, half_rows(me.high), :], other_ref)
+    groups = (me.high, 1 - me.high)
+    for d in range(1, 4):
+        to = me.beside_y(d)
+        for i, (home, group) in enumerate(zip(homes, groups)):
+            columns = head_columns(group * 4 + (me.y + d) % 4)
+            for j, ref in enumerate((k_ref, v_ref)):
+                send(
+                    ref.at[:, columns], home.at[j, head_rows(me.y), :],
+                    head_send.at[i, j, d], head_recv.at[i, j, d], own, to,
+                )
     for j, ref in enumerate((k_ref, v_ref)):
         kv_ref[own, j, head_rows(head), :] = ref[:, head_columns(head)]
+        other_ref[j, head_rows(me.y), :] = ref[:, head_columns(me.partner)]
 
     for load in loads[2:]:
         load.wait()
@@ -171,7 +188,8 @@
     lanes = lax.broadcasted_iota(jnp.int32, (1, WIDTH), 1)
     norms = norm_ref[...].astype(F32).T
     query_pos, query_start = [], []
-    for half in range(2):
+
+    def prepare(half):
         here = slice(half * BLOCK, (half + 1) * BLOCK)
         for h in range(8):
             cols = slice(h * WIDTH, (h + 1) * WIDTH)
@@ -198,57 +216,77 @@
             start = jnp.maximum(start, jnp.where(s <= pos, s, 0))
         query_pos.append(jnp.where(lanes < BLOCK, pos, 1 << 20))
         query_start.append(jnp.where(lanes < BLOCK, start, 0))
+
+    prepare(0)
     tile_lane = lax.broadcasted_iota(jnp.int32, (TILE, WIDTH), 1)
     value_extra = jnp.where(tile_lane < 3, -1.0, 0.0).astype(BF16)
     norm_extra = jnp.zeros((1, WIDTH), F32)
     for i, term in enumerate(ROOT_PARTS):
         norm_extra = jnp.where(lanes == BLOCK + i, -term, norm_extra)
 
-    for d in range(1, 8):
-        peer = (head + 8 - d) % 8
-        for j in range(2):
-            here = kv_ref.at[own, j, head_rows(peer), :]
-            copy_to(here, here, head_send.at[j, d], head_recv.at[j, d], own, peer).wait_recv()
-
-    def over(block, k, which):
-        send(block, block, s_send.at[k, which], s_recv.at[k, which], sibling, head)
-
-    def give_column(k):
+    for d in range(1, 4):
+        source = me.beside_y(4 - d)
+        for i, home in enumerate(homes):
+            for j in range(2):
+                here = home.at[j, head_rows((me.y + 4 - d) % 4), :]
+                copy_to(
+                    here, here, head_send.at[i, j, d], head_recv.at[i, j, d], own, source
+                ).wait_recv()
+
+    for i, z in enumerate(me.near_z):
+        send(homes[0], homes[0], z_send.at[0, i], z_recv.at[me.high, me.z], me.at(z), head)
+    for i, z in enumerate((me.z,) + me.near_z):
+        send(other_ref, homes[0], z_send.at[1, i], z_recv.at[me.high, me.z], me.at(z), me.partner)
+
+    def item(i, dx, other=False):
+        k, which = ITEMS[i]
+        block = kv_ref.at[me.at(order[k], dx, other)]
+        if which == ALL:
+            return block
+        return block.at[:, half_rows(me.high if which == MINE else 1 - me.high), :]
+
+    def over(block, i, which):
+        send(block, block, s_send.at[i, which], s_recv.at[i, which], sibling, head)
+
+    def give_column(i):
+        k, which = ITEMS[i]
         span = me.at(order[k])
-        block = kv_ref.at[span]
-        if k > 0:
-            arrived(block, z_recv.at[order[k]], span)
-        send(block, block, x_send.at[0, k], x_recv.at[0, k], right, head)
-        send(block, block, x_send.at[1, k], x_recv.at[1, k], left, head)
-        if k == 0:
-            for i, z in enumerate(me.near_z):
-                send(block, block, z_send.at[i], z_recv.at[me.z], me.at(z), head)
-        over(block, k, 0)
-
-    def give_beside(k):
-        block = kv_ref.at[me.at(order[k], LEFT)]
-        arrived(block, x_recv.at[0, k], left)
-        send(block.at[0], block.at[0], f_send.at[0, k], f_recv.at[0, k], right, head)
-        over(block, k, 1)
-        block = kv_ref.at[me.at(order[k], RIGHT)]
-        arrived(block, x_recv.at[1, k], right)
-        send(block.at[1], block.at[1], f_send.at[1, k], f_recv.at[1, k], left, head)
-        over(block, k, 2)
-
-    def give_far(k):
-        block = kv_ref.at[me.at(order[k], FAR)]
-        arrived(block.at[0], f_recv.at[0, k], left)
-        over(block.at[0], k, 3)
-        arrived(block.at[1], f_recv.at[1, k], right)
-        over(block.at[1], k, 4)
+        for high in (me.high, 1 - me.high):
+            if which == ALL or (which == OTHER and high is not me.high):
+                half = kv_ref.at[span, :, half_rows(high), :]
+                arrived(half, z_recv.at[high, order[k]], span)
+        block = item(i, OWN)
+        send(block, block, x_send.at[0, i], x_recv.at[0, i], right, head)
+        send(block, block, x_send.at[1, i], x_recv.at[1, i], left, head)
+        over(block, i, 0)
+
+    def give_beside(i):
+        block = item(i, LEFT)
+        arrived(block, x_recv.at[0, i], left)
+        send(block.at[0], block.at[0], f_send.at[0, i], f_recv.at[0, i], right, head)
+        over(block, i, 1)
+        block = item(i, RIGHT)
+        arrived(block, x_recv.at[1, i], right)
+        send(block.at[1], block.at[1], f_send.at[1, i], f_recv.at[1, i], left, head)
+        over(block, i, 2)
+
+    def give_far(i):
+        block = item(i, FAR)
+        arrived(block.at[0], f_recv.at[0, i], left)
+        over(block.at[0], i, 3)
+        arrived(block.at[1], f_recv.at[1, i], right)
+        over(block.at[1], i, 4)
 
     def ready(k, dx):
-        block = kv_ref.at[me.at(order[k], dx, True)]
-        if dx == FAR:
-            arrived(block.at[0], s_recv.at[k, 3], sibling)
-            arrived(block.at[1], s_recv.at[k, 4], sibling)
-        else:
-            arrived(block, s_recv.at[k, {OWN: 0, LEFT: 1, RIGHT: 2}[dx]], sibling)
+        for i, (at, _) in enumerate(ITEMS):
+            if at != k:
+                continue
+            block = item(i, dx, True)
+            if dx == FAR:
+                arrived(block.at[0], s_recv.at[i, 3], sibling)
+                arrived(block.at[1], s_recv.at[i, 4], sibling)
+            else:
+                arrived(block, s_recv.at[i, {OWN: 0, LEFT: 1, RIGHT: 2}[dx]], sibling)
 
     def pair(k, dx, j):
         step = STEP_OF[k, dx]
@@ -282,28 +320,37 @@
             pair(k, OWN, j) + near[0, k, j].astype(F32) + near[1, k, j].astype(F32)
             for j in range(2)
         ]
-        if k == 0:
-            return sums
         for j in range(2):
             deep_out[k, j] = sums[j].astype(BF16)
-        send(
-            deep_out.at[k], deep.at[me.z], rz_send.at[k], rz_recv.at[me.z], me.at(order[k]), head
-        )
+        if k == 0:
+            for j in range(2):
+                deep_sum[j] = sums[j]
+                mine_sum[j] = deep_sum[j, half_rows(me.high), :]
+        for i, to in enumerate((head, me.partner)):
+            if k > 0 or i > 0:
+                send(
+                    deep_out.at[k, :, half_rows(me.high if i == 0 else 1 - me.high), :],
+                    deep.at[me.high, me.z], rz_send.at[i, k], rz_recv.at[me.high, me.z],
+                    me.at(order[k]), to,
+                )
 
     before = {
-        0: [(give_column, 0)],
-        1: [(give_beside, 0), (give_column, 1)],
-        2: [(give_column, 2)],
-        3: [(give_far, 0)],
-        4: [(give_beside, 1), (give_column, 3)],
-        6: [(give_beside, 2), (give_far, 1)],
-        8: [(give_beside, 3), (give_far, 2)],
-        9: [(sum_far, 0)],
-        11: [(give_far, 3)],
-        13: [(sum_far, 1), (sum_beside, 0)],
-        15: [(sum_far, 2)],
+        0: [(give_beside, 0), (give_column, 1), (give_column, 2)],
+        1: [(give_column, 3), (give_far, 0)],
+        2: [(give_beside, 1), (give_column, 4), (give_beside, 2)],
+        3: [(give_far, 1)],
+        4: [(give_beside, 3), (give_far, 2)],
+        6: [(give_beside, 4), (give_far, 3)],
+        8: [(sum_far, 0)],
+        9: [(give_far, 4)],
+        11: [(sum_far, 1)],
+        12: [(sum_beside, 0)],
+        14: [(sum_far, 2)],
+        15: [(sum_far, 3), (sum_beside, 1)],
     }
     chips = [order[k] * 4 + (me.x + dx) % 4 for k, dx in UNITS]
+    give_column(0)
+    prepare(1)
     block_row = lax.broadcasted_iota(jnp.int32, (BLOCK, WIDTH), 0)
 
     def unit(step, carry):
@@ -354,44 +401,51 @@
         return carry
 
     lax.fori_loop(0, len(UNITS), unit, 0)
-    sum_beside(1)
-    sum_far(3)
+    sum_beside(2)
+    sum_column(0)
     for half in range(2):
         dq = (dq_turn[half] * SCALE).T
         for h in range(8):
             dq_ref[half * BLOCK : (half + 1) * BLOCK, h * WIDTH : (h + 1) * WIDTH] = dq[
                 h * BLOCK : (h + 1) * BLOCK
             ].astype(BF16)
-    sum_beside(2)
     sum_column(1)
     sum_beside(3)
     sum_column(2)
     sum_column(3)
-    sums = sum_column(0)
-    for z in me.near_z:
-        arrived(deep.at[z], rz_recv.at[z], me.at(z))
-        sums = [sums[j] + deep[z, j].astype(F32) for j in range(2)]
-    for j in range(2):
-        total[j] = sums[j].astype(BF16)
+    for i, group in enumerate(groups):
+        sums = None if i else [mine_sum[j] for j in range(2)]
+        for z in order[1 - i :]:
+            arrived(deep.at[group, z], rz_recv.at[group, z], me.at(z))
+            got = [deep[group, z, j].astype(F32) for j in range(2)]
+            sums = got if sums is None else [sums[j] + got[j] for j in range(2)]
+        for j in range(2):
+            total[i, j] = sums[j].astype(BF16)
     outs = (dk_ref, dv_ref)
-    for d in range(1, 8):
-        peer = (head + d) % 8
+    for d in range(1, 4):
+        for i, group in enumerate(groups):
+            columns = head_columns(group * 4 + me.y)
+            for j in range(2):
+                send(
+                    total.at[i, j, head_rows((me.y + d) % 4), :], outs[j].at[:, columns],
+                    rh_send.at[i, j, d], rh_recv.at[i, j, d], own, me.beside_y(d),
+                )
+    for i, group in enumerate(groups):
         for j in range(2):
-            send(
-                total.at[j, head_rows(peer), :], outs[j].at[:, head_columns(head)],
-                rh_send.at[j, d], rh_recv.at[j, d], own, peer,
-            )
-    for j in range(2):
-        outs[j][:, head_columns(head)] = total[j, head_rows(head), :]
-    for d in range(1, 8):
-        peer = (head + 8 - d) % 8
-        for j in range(2):
-            here = outs[j].at[:, head_columns(peer)]
-            copy_to(here, here, rh_send.at[j, d], rh_recv.at[j, d], own, peer).wait_recv()
+            outs[j][:, head_columns(group * 4 + me.y)] = total[i, j, head_rows(me.y), :]
+    for d in range(1, 4):
+        for i, group in enumerate(groups):
+            for j in range(2):
+                here = outs[j].at[:, head_columns(group * 4 + (me.y + 4 - d) % 4)]
+                copy_to(
+                    here, here, rh_send.at[i, j, d], rh_recv.at[i, j, d], own, me.beside_y(4 - d)
+                ).wait_recv()
     sent += [(sib_out.shape[1:], p_send.at[step]) for step in range(len(UNITS))]
     shapes = {
         (2, 2 * BLOCK, WIDTH): kv_ref.at[0],
         (2 * BLOCK, WIDTH): kv_ref.at[0, 0],
+        (2, BLOCK, WIDTH): other_ref,
+        (BLOCK, WIDTH): other_ref.at[0],
         (16, WIDTH): kv_ref.at[0, 0, pl.ds(0, 16), :],
     }
     for shape, sent_sem in sent:
@@ -420,6 +474,7 @@
             pltpu.VMEM(key_matrix.shape, BF16),
             pltpu.VMEM(key_matrix.shape, BF16),
             pltpu.VMEM((32, 2) + chunk, BF16),
+            pltpu.VMEM((2, BLOCK, WIDTH), BF16),
             pltpu.VMEM((2, rows, 2 * WIDTH), BF16),
             pltpu.VMEM((2, rows, 2 * WIDTH), BF16),
             pltpu.VMEM((2, 2 * WIDTH, rows), BF16),
@@ -431,16 +486,18 @@
             pltpu.VMEM((16, 2) + chunk, BF16),
             pltpu.VMEM((2, 4) + chunk, BF16),
             pltpu.VMEM((2, 4, 2) + chunk, BF16),
-            pltpu.VMEM((4, 2) + chunk, BF16),
+            pltpu.VMEM((2, 4, 2, BLOCK, WIDTH), BF16),
             pltpu.VMEM((4, 2) + chunk, BF16),
             pltpu.VMEM((2, 4, 2) + chunk, BF16),
             pltpu.VMEM((4, 2) + chunk, BF16),
-            pltpu.VMEM((2,) + chunk, BF16),
+            pltpu.VMEM((2, 2, BLOCK, WIDTH), BF16),
+            pltpu.VMEM((2,) + chunk, F32),
+            pltpu.VMEM((2, BLOCK, WIDTH), F32),
             dma((6,)),
-            dma((2, 8)), dma((2, 8)), dma((3,)), dma((4,)), dma((2, 4)), dma((2, 4)),
-            dma((2, 4)), dma((2, 4)), dma((4, 5)), dma((4, 5)),
+            dma((2, 2, 4)), dma((2, 2, 4)), dma((2, 4)), dma((2, 4)), dma((2, 5)), dma((2, 5)),
+            dma((2, 5)), dma((2, 5)), dma((5, 5)), dma((5, 5)),
             dma((16,)), dma((16,)), dma((2, 4)), dma((2, 4)), dma((2, 4)), dma((2, 4)),
-            dma((4,)), dma((4,)), dma((2, 8)), dma((2, 8)),
+            dma((2, 4)), dma((2, 4)), dma((2, 2, 4)), dma((2, 2, 4)),
         ],
         compiler_params=pltpu.CompilerParams(
             collective_id=0, has_side_effects=True, vmem_limit_bytes=56 * 2**20

time: 69 us -> 66.4 us (0.962)
  Pallas kernels: 64.7 us -> 62 us
    pallas_call x1, Pallas kernels: 64.7 us -> 62 us  [backward(): pl.pallas_call(backward_kernel, out_shape=(jax.ShapeDtypeStruct(queries.s...]
where the time goes in v4:
time: 66.4 us; the launch traced here: 65.7 us
  Pallas kernels  62 us (93%)
  local copies, waits for them, and re-layouts  3.06 us (5%)
    pallas_call x1, Pallas kernels, backward(): pl.pallas_call(backward_kernel, out_shape=(jax.ShapeDtypeStruct(queries.s...  62 us
    unnamed x7, local copies, waits for them, and re-layouts  3.06 us

profile of v4, /device:TPU:8, one launch (start us, length us, event | category | flops | bytes accessed | tf_op | source)
XLA Modules:
  0.0 65.7 jit_solution(11468449860023810282)
XLA Ops:
  0.6 62.0 %backward.1 = (bf16[128,1024]{1,0:T(8,128)(2,1)}, bf16[16,1024]{1,0:T(8,128)(2,1)}, bf16[16,1024]{1,0:T(8,128)(2,1)}) custom-call(s32[64]{0:T(128)} %order_ref.1, s32[32,128]{1,0:T(8,128)} %bitcast.2, bf16[128,1024]{1,0:T(8,128)(2,1)} %q_hbm.1, bf16[128,1024]{1,0:T(8,128)(2,1)} %o_hbm.1, bf16[128,1024]{1,0:T(8,128)(2,1)} %g_hbm.1, bf16[8,128]{1,0:T(8,128)(2,1)} %bitcast.3, ...), custom_call_target="tpu_custom_call" | custom-call | tf_op jit(solution)/shard_map/backward/pallas_call | solution.py:464
  62.6 0.0 copy-start.1
  62.6 1.7 %copy.14 = bf16[128,1024]{1,0:T(8,128)(2,1)} copy(bf16[128,1024]{1,0:T(8,128)(2,1)} %get-tuple-element.6) | data formatting | bytes 524288
  64.3 0.0 copy-done.1
  64.3 0.0 copy-start
  64.3 0.6 copy.15
  64.9 0.2 copy-done
  65.1 0.6 copy.16
Async XLA Ops:
  62.6 1.7 %copy-start.1 = (bf16[16,1024]{1,0:T(8,128)(2,1)S(1)}, bf16[16,1024]{1,0:T(8,128)(2,1)}, u32[]{:S(2)}) copy-start(bf16[16,1024]{1,0:T(8,128)(2,1)} %get-tuple-element.7) | copy-start | bytes 98308
  64.3 0.8 %copy-start = (bf16[16,1024]{1,0:T(8,128)(2,1)S(1)}, bf16[16,1024]{1,0:T(8,128)(2,1)}, u32[]{:S(2)}) copy-start(bf16[16,1024]{1,0:T(8,128)(2,1)} %get-tuple-element.8) | copy-start | bytes 98308

commit v5 on v4

--- a/solution.py
+++ b/solution.py
@@ -65,7 +65,7 @@
     peers = [(place.span, place.beside_y(d)) for d in range(1, 4)]
     peers += [(place.at(z), place.head) for z in place.near_z]
     peers += [(place.at(z), place.partner) for z in (place.z,) + place.near_z]
-    peers += [(place.at(place.z, 1), place.head), (place.at(place.z, 3), place.head)]
+    peers += [(place.at(place.z, dx), place.head) for dx in (1, 2, 3)]
     peers += [(place.sibling, place.head)]
     for peer in peers:
         pl.semaphore_signal(
@@ -109,8 +109,8 @@
 
 OWN, LEFT, RIGHT, FAR = 0, 3, 1, 2
 UNITS = [
-    (0, OWN), (1, OWN), (0, LEFT), (0, RIGHT), (2, OWN), (0, FAR), (1, LEFT), (1, RIGHT),
-    (1, FAR), (2, LEFT), (2, RIGHT), (2, FAR), (3, FAR), (3, LEFT), (3, RIGHT), (3, OWN),
+    (0, OWN), (1, OWN), (2, OWN), (0, LEFT), (0, RIGHT), (0, FAR), (1, LEFT), (1, RIGHT),
+    (1, FAR), (2, LEFT), (2, RIGHT), (2, FAR), (3, LEFT), (3, RIGHT), (3, FAR), (3, OWN),
 ]
 ALL, MINE, OTHER = 0, 1, 2
 ITEMS = [(0, MINE), (1, ALL), (0, OTHER), (2, ALL), (3, ALL)]
@@ -122,21 +122,18 @@
     dq_ref, dk_ref, dv_ref,
     docs_ref, q_ref, o_ref, g_ref, k_ref, v_ref,
     kv_ref, other_ref, q_all, g_all, q_turn, g_turn, dq_turn, work,
-    part, sib_out, sib, far, near, deep, far_out, near_out, deep_out, total, deep_sum, mine_sum,
+    part, sib_out, sib, near, deep, near_out, deep_out, total, deep_sum, mine_sum,
     load_sem,
-    head_send, head_recv, z_send, z_recv, x_send, x_recv, f_send, f_recv, s_send, s_recv,
-    p_send, p_recv, rf_send, rf_recv, rx_send, rx_recv, rz_send, rz_recv, rh_send, rh_recv,
+    head_send, head_recv, z_send, z_recv, x_send, x_recv, s_send, s_recv,
+    p_send, p_recv, rx_send, rx_recv, rz_send, rz_recv, rh_send, rh_recv,
 ):
-    (
-        head_send, z_send, x_send, f_send, s_send, p_send, rf_send, rx_send, rz_send, rh_send
-    ) = map(
-        Sent,
-        (head_send, z_send, x_send, f_send, s_send, p_send, rf_send, rx_send, rz_send, rh_send),
+    head_send, z_send, x_send, s_send, p_send, rx_send, rz_send, rh_send = map(
+        Sent, (head_send, z_send, x_send, s_send, p_send, rx_send, rz_send, rh_send)
     )
     me = Place()
     own, head = me.span, me.head
     order = (me.z,) + me.near_z
-    left, right, sibling = me.at(me.z, LEFT), me.at(me.z, RIGHT), me.sibling
+    sibling = me.sibling
 
     loads = [
         pltpu.make_async_copy(src, dst, load_sem.at[i])
@@ -233,10 +230,16 @@
                     here, here, head_send.at[i, j, d], head_recv.at[i, j, d], own, source
                 ).wait_recv()
 
-    for i, z in enumerate(me.near_z):
-        send(homes[0], homes[0], z_send.at[0, i], z_recv.at[me.high, me.z], me.at(z), head)
-    for i, z in enumerate((me.z,) + me.near_z):
-        send(other_ref, homes[0], z_send.at[1, i], z_recv.at[me.high, me.z], me.at(z), me.partner)
+    def give_deep(k):
+        if k > 0:
+            send(
+                homes[0], homes[0], z_send.at[0, k], z_recv.at[me.high, me.z],
+                me.at(order[k]), head,
+            )
+        send(
+            other_ref, homes[0], z_send.at[1, k], z_recv.at[me.high, me.z],
+            me.at(order[k]), me.partner,
+        )
 
     def item(i, dx, other=False):
         k, which = ITEMS[i]
@@ -256,37 +259,21 @@
                 half = kv_ref.at[span, :, half_rows(high), :]
                 arrived(half, z_recv.at[high, order[k]], span)
         block = item(i, OWN)
-        send(block, block, x_send.at[0, i], x_recv.at[0, i], right, head)
-        send(block, block, x_send.at[1, i], x_recv.at[1, i], left, head)
-        over(block, i, 0)
-
-    def give_beside(i):
-        block = item(i, LEFT)
-        arrived(block, x_recv.at[0, i], left)
-        send(block.at[0], block.at[0], f_send.at[0, i], f_recv.at[0, i], right, head)
-        over(block, i, 1)
-        block = item(i, RIGHT)
-        arrived(block, x_recv.at[1, i], right)
-        send(block.at[1], block.at[1], f_send.at[1, i], f_recv.at[1, i], left, head)
-        over(block, i, 2)
-
-    def give_far(i):
-        block = item(i, FAR)
-        arrived(block.at[0], f_recv.at[0, i], left)
-        over(block.at[0], i, 3)
-        arrived(block.at[1], f_recv.at[1, i], right)
-        over(block.at[1], i, 4)
+        for dx in (FAR, RIGHT, LEFT):
+            send(block, block, x_send.at[dx, i], x_recv.at[dx, i], me.at(me.z, dx), head)
+        over(block, i, OWN)
+
+    def give_on(i, *steps):
+        for dx in steps:
+            block = item(i, dx)
+            arrived(block, x_recv.at[4 - dx, i], me.at(me.z, dx))
+            over(block, i, dx)
 
     def ready(k, dx):
         for i, (at, _) in enumerate(ITEMS):
             if at != k:
                 continue
-            block = item(i, dx, True)
-            if dx == FAR:
-                arrived(block.at[0], s_recv.at[i, 3], sibling)
-                arrived(block.at[1], s_recv.at[i, 4], sibling)
-            else:
-                arrived(block, s_recv.at[i, {OWN: 0, LEFT: 1, RIGHT: 2}[dx]], sibling)
+            arrived(item(i, dx, True), s_recv.at[i, dx], sibling)
 
     def pair(k, dx, j):
         step = STEP_OF[k, dx]
@@ -296,30 +283,22 @@
         step = STEP_OF[k, dx]
         arrived(sib.at[step], p_recv.at[step], sibling)
 
-    def sum_far(k):
-        met(k, FAR)
-        for j, span in enumerate((right, left)):
-            far_out[k, j] = pair(k, FAR, j).astype(BF16)
-            send(far_out.at[k, j], far.at[j, k], rf_send.at[j, k], rf_recv.at[j, k], span, head)
-
-    def sum_beside(k):
-        for i, (dx, span, source) in enumerate(((RIGHT, right, left), (LEFT, left, right))):
-            met(k, dx)
-            arrived(far.at[i, k], rf_recv.at[i, k], source)
-            near_out[i, k, i] = (pair(k, dx, i) + far[i, k].astype(F32)).astype(BF16)
-            near_out[i, k, 1 - i] = pair(k, dx, 1 - i).astype(BF16)
-            send(
-                near_out.at[i, k], near.at[i, k], rx_send.at[i, k], rx_recv.at[i, k], span, head
-            )
+    def give_sum(step):
+        k, dx = UNITS[step]
+        met(k, dx)
+        for j in range(2):
+            near_out[dx, k, j] = pair(k, dx, j).astype(BF16)
+        send(
+            near_out.at[dx, k], near.at[dx, k], rx_send.at[dx, k], rx_recv.at[dx, k],
+            me.at(me.z, dx), head,
+        )
 
     def sum_column(k):
         met(k, OWN)
-        arrived(near.at[0, k], rx_recv.at[0, k], left)
-        arrived(near.at[1, k], rx_recv.at[1, k], right)
-        sums = [
-            pair(k, OWN, j) + near[0, k, j].astype(F32) + near[1, k, j].astype(F32)
-            for j in range(2)
-        ]
+        sums = [pair(k, OWN, j) for j in range(2)]
+        for dx in (LEFT, RIGHT, FAR):
+            arrived(near.at[dx, k], rx_recv.at[dx, k], me.at(me.z, 4 - dx))
+            sums = [sums[j] + near[dx, k, j].astype(F32) for j in range(2)]
         for j in range(2):
             deep_out[k, j] = sums[j].astype(BF16)
         if k == 0:
@@ -335,22 +314,29 @@
                 )
 
     before = {
-        0: [(give_beside, 0), (give_column, 1), (give_column, 2)],
-        1: [(give_column, 3), (give_far, 0)],
-        2: [(give_beside, 1), (give_column, 4), (give_beside, 2)],
-        3: [(give_far, 1)],
-        4: [(give_beside, 3), (give_far, 2)],
-        6: [(give_beside, 4), (give_far, 3)],
-        8: [(sum_far, 0)],
-        9: [(give_far, 4)],
-        11: [(sum_far, 1)],
-        12: [(sum_beside, 0)],
-        14: [(sum_far, 2)],
-        15: [(sum_far, 3), (sum_beside, 1)],
+        0: [(give_column, 1), (give_column, 2)],
+        1: [(give_on, 0, LEFT, RIGHT), (give_column, 3)],
+        2: [(give_on, 0, FAR), (give_column, 4)],
+        3: [(give_on, 2, LEFT, RIGHT), (give_on, 1, LEFT, RIGHT)],
+        4: [(give_on, 2, FAR), (give_on, 1, FAR)],
+        6: [(give_sum, 3)],
+        7: [(give_sum, 4), (give_on, 3, LEFT, RIGHT)],
+        8: [(give_sum, 5), (give_on, 3, FAR)],
+        9: [(give_sum, 6)],
+        10: [(give_sum, 7), (give_on, 4, LEFT, RIGHT)],
+        11: [(give_sum, 8), (give_on, 4, FAR)],
+        12: [(give_sum, 9)],
+        13: [(give_sum, 10)],
+        14: [(give_sum, 11), (sum_column, 0)],
+        15: [(give_sum, 12)],
     }
     chips = [order[k] * 4 + (me.x + dx) % 4 for k, dx in UNITS]
+    give_deep(1)
+    give_deep(0)
     give_column(0)
     prepare(1)
+    give_deep(2)
+    give_deep(3)
     block_row = lax.broadcasted_iota(jnp.int32, (BLOCK, WIDTH), 0)
 
     def unit(step, carry):
@@ -358,8 +344,8 @@
 
             @pl.when(step == at)
             def _():
-                for action, which in before.get(at, []):
-                    action(which)
+                for action, *which in before.get(at, []):
+                    action(*which)
                 ready(k, dx)
 
         chip = chips[0]
@@ -401,16 +387,15 @@
         return carry
 
     lax.fori_loop(0, len(UNITS), unit, 0)
-    sum_beside(2)
-    sum_column(0)
+    give_sum(13)
+    give_sum(14)
+    sum_column(1)
     for half in range(2):
         dq = (dq_turn[half] * SCALE).T
         for h in range(8):
             dq_ref[half * BLOCK : (half + 1) * BLOCK, h * WIDTH : (h + 1) * WIDTH] = dq[
                 h * BLOCK : (h + 1) * BLOCK
             ].astype(BF16)
-    sum_column(1)
-    sum_beside(3)
     sum_column(2)
     sum_column(3)
     for i, group in enumerate(groups):
@@ -484,19 +469,16 @@
             pltpu.VMEM((16, 2) + chunk, F32),
             pltpu.VMEM((16, 2) + chunk, BF16),
             pltpu.VMEM((16, 2) + chunk, BF16),
-            pltpu.VMEM((2, 4) + chunk, BF16),
-            pltpu.VMEM((2, 4, 2) + chunk, BF16),
+            pltpu.VMEM((4, 4, 2) + chunk, BF16),
             pltpu.VMEM((2, 4, 2, BLOCK, WIDTH), BF16),
-            pltpu.VMEM((4, 2) + chunk, BF16),
-            pltpu.VMEM((2, 4, 2) + chunk, BF16),
+            pltpu.VMEM((4, 4, 2) + chunk, BF16),
             pltpu.VMEM((4, 2) + chunk, BF16),
             pltpu.VMEM((2, 2, BLOCK, WIDTH), BF16),
             pltpu.VMEM((2,) + chunk, F32),
             pltpu.VMEM((2, BLOCK, WIDTH), F32),
             dma((6,)),
-            dma((2, 2, 4)), dma((2, 2, 4)), dma((2, 4)), dma((2, 4)), dma((2, 5)), dma((2, 5)),
-            dma((2, 5)), dma((2, 5)), dma((5, 5)), dma((5, 5)),
-            dma((16,)), dma((16,)), dma((2, 4)), dma((2, 4)), dma((2, 4)), dma((2, 4)),
+            dma((2, 2, 4)), dma((2, 2, 4)), dma((2, 4)), dma((2, 4)), dma((4, 5)), dma((4, 5)),
+            dma((5, 4)), dma((5, 4)), dma((16,)), dma((16,)), dma((4, 4)), dma((4, 4)),
             dma((2, 4)), dma((2, 4)), dma((2, 2, 4)), dma((2, 2, 4)),
         ],
         compiler_params=pltpu.CompilerParams(

time: 66.4 us -> 60.9 us (0.917)
  Pallas kernels: 62 us -> 56.9 us
    pallas_call x1, Pallas kernels: 62 us -> 56.9 us  [backward(): pl.pallas_call(backward_kernel, out_shape=(jax.ShapeDtypeStruct(queries.s...]
where the time goes in v5:
time: 60.9 us; the launch traced here: 60.6 us
  Pallas kernels  56.9 us (93%)
  local copies, waits for them, and re-layouts  3.06 us (5%)
  between operations  0.65 us (1%)
    pallas_call x1, Pallas kernels, backward(): pl.pallas_call(backward_kernel, out_shape=(jax.ShapeDtypeStruct(queries.s...  56.9 us
    unnamed x7, local copies, waits for them, and re-layouts  3.06 us

profile of v5, /device:TPU:8, one launch (start us, length us, event | category | flops | bytes accessed | tf_op | source)
XLA Modules:
  0.0 60.6 jit_solution(9748537220854481172)
XLA Ops:
  0.6 56.9 %backward.1 = (bf16[128,1024]{1,0:T(8,128)(2,1)}, bf16[16,1024]{1,0:T(8,128)(2,1)}, bf16[16,1024]{1,0:T(8,128)(2,1)}) custom-call(s32[64]{0:T(128)} %order_ref.1, s32[32,128]{1,0:T(8,128)} %bitcast.2, bf16[128,1024]{1,0:T(8,128)(2,1)} %q_hbm.1, bf16[128,1024]{1,0:T(8,128)(2,1)} %o_hbm.1, bf16[128,1024]{1,0:T(8,128)(2,1)} %g_hbm.1, bf16[8,128]{1,0:T(8,128)(2,1)} %bitcast.3, ...), custom_call_target="tpu_custom_call" | custom-call | tf_op jit(solution)/shard_map/backward/pallas_call | solution.py:449
  57.5 0.0 copy-start.1
  57.6 1.7 %copy.14 = bf16[128,1024]{1,0:T(8,128)(2,1)} copy(bf16[128,1024]{1,0:T(8,128)(2,1)} %get-tuple-element.6) | data formatting | bytes 524288
  59.2 0.0 copy-done.1
  59.2 0.0 copy-start
  59.2 0.6 %copy.15 = bf16[16,1024]{1,0:T(8,128)(2,1)} copy(bf16[16,1024]{1,0:T(8,128)(2,1)S(1)} %copy-done.1) | data formatting | bytes 65536
  59.8 0.2 copy-done
  60.0 0.6 %copy.16 = bf16[16,1024]{1,0:T(8,128)(2,1)} copy(bf16[16,1024]{1,0:T(8,128)(2,1)S(1)} %copy-done) | data formatting | bytes 65536
Async XLA Ops:
  57.5 1.7 %copy-start.1 = (bf16[16,1024]{1,0:T(8,128)(2,1)S(1)}, bf16[16,1024]{1,0:T(8,128)(2,1)}, u32[]{:S(2)}) copy-start(bf16[16,1024]{1,0:T(8,128)(2,1)} %get-tuple-element.7) | copy-start | bytes 98308
  59.2 0.8 %copy-start = (bf16[16,1024]{1,0:T(8,128)(2,1)S(1)}, bf16[16,1024]{1,0:T(8,128)(2,1)}, u32[]{:S(2)}) copy-start(bf16[16,1024]{1,0:T(8,128)(2,1)} %get-tuple-element.8) | copy-start | bytes 98308

commit v6 on v5

--- a/solution.py
+++ b/solution.py
@@ -358,23 +358,29 @@
         )
         value_side = jnp.concatenate([values, value_extra], axis=1)
         keys_turn = keys.T
-        grad_keys = grad_values = None
+        scores, grad_weights = [], []
         for half in range(2):
             hidden = (key_pos > query_pos[half]) | (key_pos < query_start[half])
             extra = jnp.where(hidden, MASKED, norm_extra).astype(BF16)
-            scores = jnp.dot(
-                jnp.concatenate([keys, extra], axis=1), q_turn[half], preferred_element_type=F32
+            scores.append(
+                jnp.dot(
+                    jnp.concatenate([keys, extra], axis=1), q_turn[half],
+                    preferred_element_type=F32,
+                )
             )
-            weights = jnp.exp2(scores * EXP2_SCALE)
-            grad_weights = jnp.dot(value_side, g_turn[half], preferred_element_type=F32)
-            grad_scores = (weights * grad_weights).astype(BF16)
-            to_values = jnp.dot(
-                weights.astype(BF16), g_all[half, :, :WIDTH], preferred_element_type=F32
-            )
-            to_keys = jnp.dot(grad_scores, q_all[half, :, :WIDTH], preferred_element_type=F32)
-            dq_turn[half] += jnp.dot(keys_turn, grad_scores, preferred_element_type=F32)
-            grad_keys = to_keys if half == 0 else grad_keys + to_keys
-            grad_values = to_values if half == 0 else grad_values + to_values
+            grad_weights.append(jnp.dot(value_side, g_turn[half], preferred_element_type=F32))
+        weights = [jnp.exp2(score * EXP2_SCALE) for score in scores]
+        grad_scores = [(weights[half] * grad_weights[half]).astype(BF16) for half in range(2)]
+        grad_values = sum(
+            jnp.dot(weights[half].astype(BF16), g_all[half, :, :WIDTH], preferred_element_type=F32)
+            for half in range(2)
+        )
+        grad_keys = sum(
+            jnp.dot(grad_scores[half], q_all[half, :, :WIDTH], preferred_element_type=F32)
+            for half in range(2)
+        )
+        for half in range(2):
+            dq_turn[half] += jnp.dot(keys_turn, grad_scores[half], preferred_element_type=F32)
         for i in range(2):
             rows = slice(2 * i * BLOCK, 2 * (i + 1) * BLOCK)
             work[i, 0] = grad_keys[rows] * SCALE
@@ -488,11 +494,33 @@
     )(order, docs, queries, output, grad_out, norm_turn, key_matrix, value_matrix)
 
 
+def hand_out_kernel(dq_ref, dk_ref, dv_ref, dq_out, dk_out, dv_out, sem):
+    pairs = ((dq_ref, dq_out), (dk_ref, dk_out), (dv_ref, dv_out))
+    copies = [pltpu.make_async_copy(src, dst, sem.at[i]) for i, (src, dst) in enumerate(pairs)]
+    for copy in copies:
+        copy.start()
+    for copy in copies:
+        copy.wait()
+
+
+def hand_out(*grads):
+    hbm = pl.BlockSpec(memory_space=pl.ANY)
+    return pl.pallas_call(
+        hand_out_kernel,
+        out_shape=tuple(jax.ShapeDtypeStruct(grad.shape, grad.dtype) for grad in grads),
+        in_specs=[pl.BlockSpec(memory_space=pltpu.VMEM)] * 3,
+        out_specs=(hbm,) * 3,
+        scratch_shapes=[pltpu.SemaphoreType.DMA((3,))],
+        name="hand_out",
+    )(*grads)
+
+
 def body(queries, key_matrix, value_matrix, output, grad_out, log_norm, doc_ids, block_order):
-    return backward(
+    grads = backward(
         block_order, doc_ids.reshape(-1, WIDTH), queries, output, grad_out, log_norm.T,
         key_matrix, value_matrix,
     )
+    return hand_out(*grads)
 
 
 def solution(mesh):

time: 60.9 us -> 57.2 us (0.939)
  local copies, waits for them, and re-layouts: 3.06 us -> 0 us
    unnamed x7 -> x0, local copies, waits for them, and re-layouts: 3.06 us -> none
    pallas_call x1, Pallas kernels: 56.9 us -> 54.7 us  [backward(): pl.pallas_call(backward_kernel, out_shape=(jax.ShapeDtypeStruct(queries.s...]
    pallas_call x0 -> x1, Pallas kernels: none -> 1.71 us  [hand_out(): pl.pallas_call(hand_out_kernel, out_shape=tuple((jax.ShapeDtypeStruct(gra...]
where the time goes in v6:
time: 57.2 us; the launch traced here: 57 us
  Pallas kernels  56.4 us (99%)
  between operations  0.64 us (1%)
    pallas_call x1, Pallas kernels, backward(): pl.pallas_call(backward_kernel, out_shape=(jax.ShapeDtypeStruct(queries.s...  54.7 us
    pallas_call x1, Pallas kernels, hand_out(): pl.pallas_call(hand_out_kernel, out_shape=tuple((jax.ShapeDtypeStruct(gra...  1.71 us

profile of v6, /device:TPU:8, one launch (start us, length us, event | category | flops | bytes accessed | tf_op | source)
XLA Modules:
  0.0 57.0 jit_solution(15136224487581375055)
XLA Ops:
  0.6 54.7 %backward.1 = (bf16[128,1024]{1,0:T(8,128)(2,1)}, bf16[16,1024]{1,0:T(8,128)(2,1)}, bf16[16,1024]{1,0:T(8,128)(2,1)}) custom-call(s32[64]{0:T(128)} %order_ref.1, s32[32,128]{1,0:T(8,128)} %bitcast.2, bf16[128,1024]{1,0:T(8,128)(2,1)} %q_hbm.1, bf16[128,1024]{1,0:T(8,128)(2,1)} %o_hbm.1, bf16[128,1024]{1,0:T(8,128)(2,1)} %g_hbm.1, bf16[8,128]{1,0:T(8,128)(2,1)} %bitcast.3, ...), custom_call_target="tpu_custom_call" | custom-call | tf_op jit(solution)/shard_map/backward/pallas_call | solution.py:455
  55.3 1.7 %hand_out.1 = (bf16[128,1024]{1,0:T(8,128)(2,1)}, bf16[16,1024]{1,0:T(8,128)(2,1)}, bf16[16,1024]{1,0:T(8,128)(2,1)}) custom-call(bf16[128,1024]{1,0:T(8,128)(2,1)} %get-tuple-element.6.dq_ref, bf16[16,1024]{1,0:T(8,128)(2,1)} %get-tuple-element.7.dk_ref, bf16[16,1024]{1,0:T(8,128)(2,1)} %get-tuple-element.8.dv_ref), custom_call_target="tpu_custom_call" | custom-call | tf_op jit(solution)/shard_map/hand_out/pallas_call | solution.py:508

commit v7 on v6

--- a/solution.py
+++ b/solution.py
@@ -71,7 +71,7 @@
         pl.semaphore_signal(
             barrier, inc=1, device_id=peer, device_id_type=pl.DeviceIdType.MESH
         )
-    pl.semaphore_wait(barrier, len(peers))
+    return lambda: pl.semaphore_wait(barrier, len(peers))
 
 
 class Sent:
@@ -135,6 +135,7 @@
     order = (me.z,) + me.near_z
     sibling = me.sibling
 
+    all_here = meet(me)
     loads = [
         pltpu.make_async_copy(src, dst, load_sem.at[i])
         for i, (src, dst) in enumerate(
@@ -146,7 +147,7 @@
     ]
     for load in loads:
         load.start()
-    meet(me)
+    all_here()
     loads[0].wait()
     loads[1].wait()
 
@@ -174,6 +175,119 @@
         kv_ref[own, j, head_rows(head), :] = ref[:, head_columns(head)]
         other_ref[j, head_rows(me.y), :] = ref[:, head_columns(me.partner)]
 
+    for d in range(1, 4):
+        source = me.beside_y(4 - d)
+        for i, home in enumerate(homes):
+            for j in range(2):
+                here = home.at[j, head_rows((me.y + 4 - d) % 4), :]
+                copy_to(
+                    here, here, head_send.at[i, j, d], head_recv.at[i, j, d], own, source
+                ).wait_recv()
+
+    def give_deep(k):
+        if k > 0:
+            send(
+                homes[0], homes[0], z_send.at[0, k], z_recv.at[me.high, me.z],
+                me.at(order[k]), head,
+            )
+        send(
+            other_ref, homes[0], z_send.at[1, k], z_recv.at[me.high, me.z],
+            me.at(order[k]), me.partner,
+        )
+
+    def item(i, dx, other=False):
+        k, which = ITEMS[i]
+        block = kv_ref.at[me.at(order[k], dx, other)]
+        if which == ALL:
+            return block
+        return block.at[:, half_rows(me.high if which == MINE else 1 - me.high), :]
+
+    def over(block, i, which):
+        send(block, block, s_send.at[i, which], s_recv.at[i, which], sibling, head)
+
+    def give_column(i):
+        k, which = ITEMS[i]
+        span = me.at(order[k])
+        for high in (me.high, 1 - me.high):
+            if which == ALL or (which == OTHER and high is not me.high):
+                half = kv_ref.at[span, :, half_rows(high), :]
+                arrived(half, z_recv.at[high, order[k]], span)
+        block = item(i, OWN)
+        for dx in (FAR, RIGHT, LEFT):
+            send(block, block, x_send.at[dx, i], x_recv.at[dx, i], me.at(me.z, dx), head)
+        over(block, i, OWN)
+
+    def give_on(i, *steps):
+        for dx in steps:
+            block = item(i, dx)
+            arrived(block, x_recv.at[4 - dx, i], me.at(me.z, dx))
+            over(block, i, dx)
+
+    def ready(k, dx):
+        for i, (at, _) in enumerate(ITEMS):
+            if at != k:
+                continue
+            arrived(item(i, dx, True), s_recv.at[i, dx], sibling)
+
+    def pair(k, dx, j):
+        step = STEP_OF[k, dx]
+        return part[step, j] + sib[step, j].astype(F32)
+
+    def met(k, dx):
+        step = STEP_OF[k, dx]
+        arrived(sib.at[step], p_recv.at[step], sibling)
+
+    def give_sum(step):
+        k, dx = UNITS[step]
+        met(k, dx)
+        for j in range(2):
+            near_out[dx, k, j] = pair(k, dx, j).astype(BF16)
+        send(
+            near_out.at[dx, k], near.at[dx, k], rx_send.at[dx, k], rx_recv.at[dx, k],
+            me.at(me.z, dx), head,
+        )
+
+    def sum_column(k):
+        met(k, OWN)
+        sums = [pair(k, OWN, j) for j in range(2)]
+        for dx in (LEFT, RIGHT, FAR):
+            arrived(near.at[dx, k], rx_recv.at[dx, k], me.at(me.z, 4 - dx))
+            sums = [sums[j] + near[dx, k, j].astype(F32) for j in range(2)]
+        for j in range(2):
+            deep_out[k, j] = sums[j].astype(BF16)
+        if k == 0:
+            for j in range(2):
+                deep_sum[j] = sums[j]
+                mine_sum[j] = deep_sum[j, half_rows(me.high), :]
+        for i, to in enumerate((head, me.partner)):
+            if k > 0 or i > 0:
+                send(
+                    deep_out.at[k, :, half_rows(me.high if i == 0 else 1 - me.high), :],
+                    deep.at[me.high, me.z], rz_send.at[i, k], rz_recv.at[me.high, me.z],
+                    me.at(order[k]), to,
+                )
+
+    before = {
+        0: [(give_column, 1), (give_column, 2)],
+        1: [(give_on, 0, LEFT, RIGHT), (give_column, 3)],
+        2: [(give_on, 0, FAR), (give_column, 4)],
+        3: [(give_on, 2, LEFT, RIGHT), (give_on, 1, LEFT, RIGHT)],
+        4: [(give_on, 2, FAR), (give_on, 1, FAR)],
+        6: [(give_sum, 3)],
+        7: [(give_sum, 4), (give_on, 3, LEFT, RIGHT)],
+        8: [(give_sum, 5), (give_on, 3, FAR)],
+        9: [(give_sum, 6)],
+        10: [(give_sum, 7), (give_on, 4, LEFT, RIGHT)],
+        11: [(give_sum, 8), (give_on, 4, FAR)],
+        12: [(give_sum, 9)],
+        13: [(give_sum, 10)],
+        14: [(give_sum, 11), (sum_column, 0)],
+        15: [(give_sum, 12)],
+    }
+    chips = [order[k] * 4 + (me.x + dx) % 4 for k, dx in UNITS]
+    give_deep(1)
+    give_deep(0)
+    give_column(0)
     for load in loads[2:]:
         load.wait()
     docs = docs_ref[...]
@@ -215,128 +329,15 @@
         query_start.append(jnp.where(lanes < BLOCK, start, 0))
 
     prepare(0)
+    give_deep(2)
+    give_deep(3)
+    prepare(1)
     tile_lane = lax.broadcasted_iota(jnp.int32, (TILE, WIDTH), 1)
     value_extra = jnp.where(tile_lane < 3, -1.0, 0.0).astype(BF16)
     norm_extra = jnp.zeros((1, WIDTH), F32)
     for i, term in enumerate(ROOT_PARTS):
         norm_extra = jnp.where(lanes == BLOCK + i, -term, norm_extra)
 
-    for d in range(1, 4):
-        source = me.beside_y(4 - d)
-        for i, home in enumerate(homes):
-            for j in range(2):
-                here = home.at[j, head_rows((me.y + 4 - d) % 4), :]
-                copy_to(
-                    here, here, head_send.at[i, j, d], head_recv.at[i, j, d], own, source
-                ).wait_recv()
-
-    def give_deep(k):
-        if k > 0:
-            send(
-                homes[0], homes[0], z_send.at[0, k], z_recv.at[me.high, me.z],
-                me.at(order[k]), head,
-            )
-        send(
-            other_ref, homes[0], z_send.at[1, k], z_recv.at[me.high, me.z],
-            me.at(order[k]), me.partner,
-        )
-
-    def item(i, dx, other=False):
-        k, which = ITEMS[i]
-        block = kv_ref.at[me.at(order[k], dx, other)]
-        if which == ALL:
-            return block
-        return block.at[:, half_rows(me.high if which == MINE else 1 - me.high), :]
-
-    def over(block, i, which):
-        send(block, block, s_send.at[i, which], s_recv.at[i, which], sibling, head)
-
-    def give_column(i):
-        k, which = ITEMS[i]
-        span = me.at(order[k])
-        for high in (me.high, 1 - me.high):
-            if which == ALL or (which == OTHER and high is not me.high):
-                half = kv_ref.at[span, :, half_rows(high), :]
-                arrived(half, z_recv.at[high, order[k]], span)
-        block = item(i, OWN)
-        for dx in (FAR, RIGHT, LEFT):
-            send(block, block, x_send.at[dx, i], x_recv.at[dx, i], me.at(me.z, dx), head)
-        over(block, i, OWN)
-
-    def give_on(i, *steps):
-        for dx in steps:
-            block = item(i, dx)
-            arrived(block, x_recv.at[4 - dx, i], me.at(me.z, dx))
-            over(block, i, dx)
-
-    def ready(k, dx):
-        for i, (at, _) in enumerate(ITEMS):
-            if at != k:
-                continue
-            arrived(item(i, dx, True), s_recv.at[i, dx], sibling)
-
-    def pair(k, dx, j):
-        step = STEP_OF[k, dx]
-        return part[step, j] + sib[step, j].astype(F32)
-
-    def met(k, dx):
-        step = STEP_OF[k, dx]
-        arrived(sib.at[step], p_recv.at[step], sibling)
-
-    def give_sum(step):
-        k, dx = UNITS[step]
-        met(k, dx)
-        for j in range(2):
-            near_out[dx, k, j] = pair(k, dx, j).astype(BF16)
-        send(
-            near_out.at[dx, k], near.at[dx, k], rx_send.at[dx, k], rx_recv.at[dx, k],
-            me.at(me.z, dx), head,
-        )
-
-    def sum_column(k):
-        met(k, OWN)
-        sums = [pair(k, OWN, j) for j in range(2)]
-        for dx in (LEFT, RIGHT, FAR):
-            arrived(near.at[dx, k], rx_recv.at[dx, k], me.at(me.z, 4 - dx))
-            sums = [sums[j] + near[dx, k, j].astype(F32) for j in range(2)]
-        for j in range(2):
-            deep_out[k, j] = sums[j].astype(BF16)
-        if k == 0:
-            for j in range(2):
-                deep_sum[j] = sums[j]
-                mine_sum[j] = deep_sum[j, half_rows(me.high), :]
-        for i, to in enumerate((head, me.partner)):
-            if k > 0 or i > 0:
-                send(
-                    deep_out.at[k, :, half_rows(me.high if i == 0 else 1 - me.high), :],
-                    deep.at[me.high, me.z], rz_send.at[i, k], rz_recv.at[me.high, me.z],
-                    me.at(order[k]), to,
-                )
-
-    before = {
-        0: [(give_column, 1), (give_column, 2)],
-        1: [(give_on, 0, LEFT, RIGHT), (give_column, 3)],
-        2: [(give_on, 0, FAR), (give_column, 4)],
-        3: [(give_on, 2, LEFT, RIGHT), (give_on, 1, LEFT, RIGHT)],
-        4: [(give_on, 2, FAR), (give_on, 1, FAR)],
-        6: [(give_sum, 3)],
-        7: [(give_sum, 4), (give_on, 3, LEFT, RIGHT)],
-        8: [(give_sum, 5), (give_on, 3, FAR)],
-        9: [(give_sum, 6)],
-        10: [(give_sum, 7), (give_on, 4, LEFT, RIGHT)],
-        11: [(give_sum, 8), (give_on, 4, FAR)],
-        12: [(give_sum, 9)],
-        13: [(give_sum, 10)],
-        14: [(give_sum, 11), (sum_column, 0)],
-        15: [(give_sum, 12)],
-    }
-    chips = [order[k] * 4 + (me.x + dx) % 4 for k, dx in UNITS]
-    give_deep(1)
-    give_deep(0)
-    give_column(0)
-    prepare(1)
-    give_deep(2)
-    give_deep(3)
     block_row = lax.broadcasted_iota(jnp.int32, (BLOCK, WIDTH), 0)
 
     def unit(step, carry):
@@ -358,7 +359,7 @@
         )
         value_side = jnp.concatenate([values, value_extra], axis=1)
         keys_turn = keys.T
-        scores, grad_weights = [], []
+        scores = []
         for half in range(2):
             hidden = (key_pos > query_pos[half]) | (key_pos < query_start[half])
             extra = jnp.where(hidden, MASKED, norm_extra).astype(BF16)
@@ -368,13 +369,15 @@
                     preferred_element_type=F32,
                 )
             )
-            grad_weights.append(jnp.dot(value_side, g_turn[half], preferred_element_type=F32))
         weights = [jnp.exp2(score * EXP2_SCALE) for score in scores]
-        grad_scores = [(weights[half] * grad_weights[half]).astype(BF16) for half in range(2)]
+        grad_weights = [
+            jnp.dot(value_side, g_turn[half], preferred_element_type=F32) for half in range(2)
+        ]
         grad_values = sum(
             jnp.dot(weights[half].astype(BF16), g_all[half, :, :WIDTH], preferred_element_type=F32)
             for half in range(2)
         )
+        grad_scores = [(weights[half] * grad_weights[half]).astype(BF16) for half in range(2)]
         grad_keys = sum(
             jnp.dot(grad_scores[half], q_all[half, :, :WIDTH], preferred_element_type=F32)
             for half in range(2)

time: 57.2 us -> 57.3 us (level)
  no operation moved by 1% of the time
where the time goes in v7:
time: 57.3 us; the launch traced here: 57.2 us
  Pallas kernels  56.5 us (99%)
  between operations  0.64 us (1%)
    pallas_call x1, Pallas kernels, backward(): pl.pallas_call(backward_kernel, out_shape=(jax.ShapeDtypeStruct(queries.s...  54.8 us
    pallas_call x1, Pallas kernels, hand_out(): pl.pallas_call(hand_out_kernel, out_shape=tuple((jax.ShapeDtypeStruct(gra...  1.71 us

profile of v7, /device:TPU:8, one launch (start us, length us, event | category | flops | bytes accessed | tf_op | source)
XLA Modules:
  0.0 57.2 jit_solution(6503763153802929439)
XLA Ops:
  0.6 54.8 %backward.1 = (bf16[128,1024]{1,0:T(8,128)(2,1)}, bf16[16,1024]{1,0:T(8,128)(2,1)}, bf16[16,1024]{1,0:T(8,128)(2,1)}) custom-call(s32[64]{0:T(128)} %order_ref.1, s32[32,128]{1,0:T(8,128)} %bitcast.2, bf16[128,1024]{1,0:T(8,128)(2,1)} %q_hbm.1, bf16[128,1024]{1,0:T(8,128)(2,1)} %o_hbm.1, bf16[128,1024]{1,0:T(8,128)(2,1)} %g_hbm.1, bf16[8,128]{1,0:T(8,128)(2,1)} %bitcast.3, ...), custom_call_target="tpu_custom_call" | custom-call | tf_op jit(solution)/shard_map/backward/pallas_call | solution.py:458
  55.4 1.7 %hand_out.1 = (bf16[128,1024]{1,0:T(8,128)(2,1)}, bf16[16,1024]{1,0:T(8,128)(2,1)}, bf16[16,1024]{1,0:T(8,128)(2,1)}) custom-call(bf16[128,1024]{1,0:T(8,128)(2,1)} %get-tuple-element.6.dq_ref, bf16[16,1024]{1,0:T(8,128)(2,1)} %get-tuple-element.7.dk_ref, bf16[16,1024]{1,0:T(8,128)(2,1)} %get-tuple-element.8.dv_ref), custom_call_target="tpu_custom_call" | custom-call | tf_op jit(solution)/shard_map/hand_out/pallas_call | solution.py:511

commit v8 on v6

--- a/solution.py
+++ b/solution.py
@@ -319,16 +319,17 @@
         2: [(give_on, 0, FAR), (give_column, 4)],
         3: [(give_on, 2, LEFT, RIGHT), (give_on, 1, LEFT, RIGHT)],
         4: [(give_on, 2, FAR), (give_on, 1, FAR)],
-        6: [(give_sum, 3)],
-        7: [(give_sum, 4), (give_on, 3, LEFT, RIGHT)],
-        8: [(give_sum, 5), (give_on, 3, FAR)],
-        9: [(give_sum, 6)],
-        10: [(give_sum, 7), (give_on, 4, LEFT, RIGHT)],
-        11: [(give_sum, 8), (give_on, 4, FAR)],
-        12: [(give_sum, 9)],
-        13: [(give_sum, 10)],
-        14: [(give_sum, 11), (sum_column, 0)],
-        15: [(give_sum, 12)],
+        5: [(give_sum, 3)],
+        6: [(give_sum, 4)],
+        7: [(give_sum, 5), (give_on, 3, LEFT, RIGHT)],
+        8: [(give_sum, 6), (give_on, 3, FAR)],
+        9: [(give_sum, 7)],
+        10: [(give_sum, 8), (give_on, 4, LEFT, RIGHT)],
+        11: [(give_sum, 9), (give_on, 4, FAR)],
+        12: [(give_sum, 10)],
+        13: [(give_sum, 11), (sum_column, 0)],
+        14: [(give_sum, 12)],
+        15: [(give_sum, 13), (sum_column, 1)],
     }
     chips = [order[k] * 4 + (me.x + dx) % 4 for k, dx in UNITS]
     give_deep(1)
@@ -393,16 +394,14 @@
         return carry
 
     lax.fori_loop(0, len(UNITS), unit, 0)
-    give_sum(13)
     give_sum(14)
-    sum_column(1)
+    sum_column(2)
     for half in range(2):
         dq = (dq_turn[half] * SCALE).T
         for h in range(8):
             dq_ref[half * BLOCK : (half + 1) * BLOCK, h * WIDTH : (h + 1) * WIDTH] = dq[
                 h * BLOCK : (h + 1) * BLOCK
             ].astype(BF16)
-    sum_column(2)
     sum_column(3)
     for i, group in enumerate(groups):
         sums = None if i else [mine_sum[j] for j in range(2)]

time: 57.2 us -> 56.4 us (0.986)
  Pallas kernels: 56.4 us -> 55.6 us
    pallas_call x1, Pallas kernels: 54.7 us -> 53.9 us  [backward(): pl.pallas_call(backward_kernel, out_shape=(jax.ShapeDtypeStruct(queries.s...]
where the time goes in v8:
time: 56.4 us; the launch traced here: 56.3 us
  Pallas kernels  55.6 us (99%)
  between operations  0.64 us (1%)
    pallas_call x1, Pallas kernels, backward(): pl.pallas_call(backward_kernel, out_shape=(jax.ShapeDtypeStruct(queries.s...  53.9 us
    pallas_call x1, Pallas kernels, hand_out(): pl.pallas_call(hand_out_kernel, out_shape=tuple((jax.ShapeDtypeStruct(gra...  1.71 us

profile of v8, /device:TPU:8, one launch (start us, length us, event | category | flops | bytes accessed | tf_op | source)
XLA Modules:
  0.0 56.3 jit_solution(9269707206923535524)
XLA Ops:
  0.6 53.9 %backward.1 = (bf16[128,1024]{1,0:T(8,128)(2,1)}, bf16[16,1024]{1,0:T(8,128)(2,1)}, bf16[16,1024]{1,0:T(8,128)(2,1)}) custom-call(s32[64]{0:T(128)} %order_ref.1, s32[32,128]{1,0:T(8,128)} %bitcast.2, bf16[128,1024]{1,0:T(8,128)(2,1)} %q_hbm.1, bf16[128,1024]{1,0:T(8,128)(2,1)} %o_hbm.1, bf16[128,1024]{1,0:T(8,128)(2,1)} %g_hbm.1, bf16[8,128]{1,0:T(8,128)(2,1)} %bitcast.3, ...), custom_call_target="tpu_custom_call" | custom-call | tf_op jit(solution)/shard_map/backward/pallas_call | solution.py:454
  54.5 1.7 %hand_out.1 = (bf16[128,1024]{1,0:T(8,128)(2,1)}, bf16[16,1024]{1,0:T(8,128)(2,1)}, bf16[16,1024]{1,0:T(8,128)(2,1)}) custom-call(bf16[128,1024]{1,0:T(8,128)(2,1)} %get-tuple-element.6.dq_ref, bf16[16,1024]{1,0:T(8,128)(2,1)} %get-tuple-element.7.dk_ref, bf16[16,1024]{1,0:T(8,128)(2,1)} %get-tuple-element.8.dv_ref), custom_call_target="tpu_custom_call" | custom-call | tf_op jit(solution)/shard_map/hand_out/pallas_call | solution.py:507

commit v9 on v7

--- a/solution.py
+++ b/solution.py
@@ -273,16 +273,17 @@
         2: [(give_on, 0, FAR), (give_column, 4)],
         3: [(give_on, 2, LEFT, RIGHT), (give_on, 1, LEFT, RIGHT)],
         4: [(give_on, 2, FAR), (give_on, 1, FAR)],
-        6: [(give_sum, 3)],
-        7: [(give_sum, 4), (give_on, 3, LEFT, RIGHT)],
-        8: [(give_sum, 5), (give_on, 3, FAR)],
-        9: [(give_sum, 6)],
-        10: [(give_sum, 7), (give_on, 4, LEFT, RIGHT)],
-        11: [(give_sum, 8), (give_on, 4, FAR)],
-        12: [(give_sum, 9)],
-        13: [(give_sum, 10)],
-        14: [(give_sum, 11), (sum_column, 0)],
-        15: [(give_sum, 12)],
+        5: [(give_sum, 3)],
+        6: [(give_sum, 4)],
+        7: [(give_sum, 5), (give_on, 3, LEFT, RIGHT)],
+        8: [(give_sum, 6), (give_on, 3, FAR)],
+        9: [(give_sum, 7)],
+        10: [(give_sum, 8), (give_on, 4, LEFT, RIGHT)],
+        11: [(give_sum, 9), (give_on, 4, FAR)],
+        12: [(give_sum, 10)],
+        13: [(give_sum, 11), (sum_column, 0)],
+        14: [(give_sum, 12)],
+        15: [(give_sum, 13), (sum_column, 1)],
     }
     chips = [order[k] * 4 + (me.x + dx) % 4 for k, dx in UNITS]
     give_deep(1)
@@ -359,7 +360,7 @@
         )
         value_side = jnp.concatenate([values, value_extra], axis=1)
         keys_turn = keys.T
-        scores = []
+        scores, grad_weights = [], []
         for half in range(2):
             hidden = (key_pos > query_pos[half]) | (key_pos < query_start[half])
             extra = jnp.where(hidden, MASKED, norm_extra).astype(BF16)
@@ -369,15 +370,13 @@
                     preferred_element_type=F32,
                 )
             )
+            grad_weights.append(jnp.dot(value_side, g_turn[half], preferred_element_type=F32))
         weights = [jnp.exp2(score * EXP2_SCALE) for score in scores]
-        grad_weights = [
-            jnp.dot(value_side, g_turn[half], preferred_element_type=F32) for half in range(2)
-        ]
+        grad_scores = [(weights[half] * grad_weights[half]).astype(BF16) for half in range(2)]
         grad_values = sum(
             jnp.dot(weights[half].astype(BF16), g_all[half, :, :WIDTH], preferred_element_type=F32)
             for half in range(2)
         )
-        grad_scores = [(weights[half] * grad_weights[half]).astype(BF16) for half in range(2)]
         grad_keys = sum(
             jnp.dot(grad_scores[half], q_all[half, :, :WIDTH], preferred_element_type=F32)
             for half in range(2)
@@ -396,16 +395,14 @@
         return carry
 
     lax.fori_loop(0, len(UNITS), unit, 0)
-    give_sum(13)
     give_sum(14)
-    sum_column(1)
+    sum_column(2)
     for half in range(2):
         dq = (dq_turn[half] * SCALE).T
         for h in range(8):
             dq_ref[half * BLOCK : (half + 1) * BLOCK, h * WIDTH : (h + 1) * WIDTH] = dq[
                 h * BLOCK : (h + 1) * BLOCK
             ].astype(BF16)
-    sum_column(2)
     sum_column(3)
     for i, group in enumerate(groups):
         sums = None if i else [mine_sum[j] for j in range(2)]

time: 57.3 us -> 56.4 us (0.984)
  Pallas kernels: 56.5 us -> 55.6 us
    pallas_call x1, Pallas kernels: 54.8 us -> 53.9 us  [backward(): pl.pallas_call(backward_kernel, out_shape=(jax.ShapeDtypeStruct(queries.s...]
where the time goes in v9:
time: 56.4 us; the launch traced here: 56.3 us
  Pallas kernels  55.6 us (99%)
  between operations  0.64 us (1%)
    pallas_call x1, Pallas kernels, backward(): pl.pallas_call(backward_kernel, out_shape=(jax.ShapeDtypeStruct(queries.s...  53.9 us
    pallas_call x1, Pallas kernels, hand_out(): pl.pallas_call(hand_out_kernel, out_shape=tuple((jax.ShapeDtypeStruct(gra...  1.71 us

profile of v9, /device:TPU:8, one launch (start us, length us, event | category | flops | bytes accessed | tf_op | source)
XLA Modules:
  0.0 56.3 jit_solution(6858795743674070057)
XLA Ops:
  0.6 53.9 %backward.1 = (bf16[128,1024]{1,0:T(8,128)(2,1)}, bf16[16,1024]{1,0:T(8,128)(2,1)}, bf16[16,1024]{1,0:T(8,128)(2,1)}) custom-call(s32[64]{0:T(128)} %order_ref.1, s32[32,128]{1,0:T(8,128)} %bitcast.2, bf16[128,1024]{1,0:T(8,128)(2,1)} %q_hbm.1, bf16[128,1024]{1,0:T(8,128)(2,1)} %o_hbm.1, bf16[128,1024]{1,0:T(8,128)(2,1)} %g_hbm.1, bf16[8,128]{1,0:T(8,128)(2,1)} %bitcast.3, ...), custom_call_target="tpu_custom_call" | custom-call | tf_op jit(solution)/shard_map/backward/pallas_call | solution.py:455
  54.5 1.7 %hand_out.1 = (bf16[128,1024]{1,0:T(8,128)(2,1)}, bf16[16,1024]{1,0:T(8,128)(2,1)}, bf16[16,1024]{1,0:T(8,128)(2,1)}) custom-call(bf16[128,1024]{1,0:T(8,128)(2,1)} %get-tuple-element.6.dq_ref, bf16[16,1024]{1,0:T(8,128)(2,1)} %get-tuple-element.7.dk_ref, bf16[16,1024]{1,0:T(8,128)(2,1)} %get-tuple-element.8.dv_ref), custom_call_target="tpu_custom_call" | custom-call | tf_op jit(solution)/shard_map/hand_out/pallas_call | solution.py:508
